TPU v7x, 128 devices: a whole 4x4x4 slice. The times are simulated.
128 devices in a mesh: section: 4 (over y_lo, core), seq: 32 (over x, y_hi, z).
Axes of the slice: x: 4, y: 4 (y_hi: 2, y_lo: 2; y = y_hi * 2 + y_lo), z: 4, core: 2. Of those that a mesh axis runs over, the one named last changes fastest.
Arguments:
- acts: bfloat16 [4, 4096, 4096], P('section', 'seq'), may hold values from -40 to 40
- gains: float32 [4, 4096], P('section'), may hold values from 0.5 to 1.5
- grad_top: bfloat16 [4096, 4096], P('seq'), may hold values from -6 to 6
- keys: bfloat16 [3072, 4096], P('seq'), may hold values from -40 to 40
- values: bfloat16 [3072, 4096], P('seq'), may hold values from -6 to 6
- offsets: int32 [32], replicated, may hold values from 0 to 2944
Outputs:
- grad_acts: bfloat16 [4, 4096, 4096], P('section', 'seq')
- grad_keys: bfloat16 [3072, 4096], P('seq')
- grad_values: bfloat16 [3072, 4096], P('seq')
All inputs are finite; a program needn't handle non-finite values.
Results may differ from a plain program's by a relative error of at most 0.015.
Values may be sent and summed in bfloat16 or wider, within the bound.
A program may use at most 128 MiB of HBM per device.

v0:
```python
import jax
import jax.numpy as jnp
from jax import lax
from jax.sharding import PartitionSpec as P

DH = 128


def passed_along(value, axis, steps):
    count = lax.axis_size(axis)
    initial, last = (max(0, -steps), min(count, count - steps))
    return lax.ppermute(value, axis, [(source, source + steps) for source in range(initial, last)])


def block_grads(query, upstream, key_heads, value_heads, positions):
    rows = query.shape[0]
    width = query.shape[1]
    count = width // DH
    klen = key_heads.shape[0]
    scale = 1.0 / DH**0.5
    query_heads = query.reshape(rows, count, DH)
    up_heads = upstream.reshape(rows, count, DH)
    scores = (
        jnp.einsum("rhd,khd->hrk", query_heads, key_heads, preferred_element_type=jnp.float32)
        * scale
    )
    allowed = jnp.arange(klen, dtype=jnp.int32)[None, None, :] <= positions[None, :, None]
    scores = jnp.where(allowed, scores, -1e30)
    peak = jnp.max(scores, axis=2, keepdims=True)
    weights = jnp.where(allowed, jnp.exp(scores - peak), 0.0)
    probs = weights / jnp.sum(weights, axis=2, keepdims=True)
    probs_round = probs.astype(jnp.bfloat16)
    dprobs = jnp.einsum("rhd,khd->hrk", up_heads, value_heads, preferred_element_type=jnp.float32)
    delta = jnp.sum(probs * dprobs, axis=2, keepdims=True)
    dscore = (probs * (dprobs - delta) * scale).astype(jnp.bfloat16)
    dquery = jnp.einsum("hrk,khd->rhd", dscore, key_heads, preferred_element_type=jnp.float32)
    dkey = jnp.einsum("hrk,rhd->khd", dscore, query_heads, preferred_element_type=jnp.float32)
    dvalue = jnp.einsum("hrk,rhd->khd", probs_round, up_heads, preferred_element_type=jnp.float32)
    return (dquery.reshape(rows, width), dkey.reshape(klen, width), dvalue.reshape(klen, width))


def layer_step(query, upstream, positions, gain_row, key_heads, value_heads, acc_keys, acc_values):
    rows = query.shape[0]
    width = query.shape[1]
    block = min(512, rows)
    nblocks = rows // block

    def one_block(carry, items):
        q_rows, up_rows, pos_rows = items
        dquery, dkey, dvalue = block_grads(q_rows, up_rows, key_heads, value_heads, pos_rows)
        return ((carry[0] + dkey, carry[1] + dvalue), dquery)

    items = (
        query.reshape(nblocks, block, width),
        upstream.reshape(nblocks, block, width),
        positions.reshape(nblocks, block),
    )
    totals, dquery = lax.scan(one_block, (acc_keys, acc_values), items)
    dquery = dquery.reshape(rows, width)
    grad_in = (upstream.astype(jnp.float32) + gain_row[None, :] * dquery).astype(jnp.bfloat16)
    return (grad_in, totals[0], totals[1])


def local(acts, gains, grad_top, keys, values, offsets):
    n_section = lax.axis_size("section")
    tq_rows = acts.shape[1]
    head_acts, head_top, head_keys, head_values = (
        lax.all_to_all(acts[0], "seq", split_axis=1, concat_axis=0, tiled=True),
        lax.all_to_all(grad_top, "seq", split_axis=1, concat_axis=0, tiled=True),
        lax.all_to_all(keys, "seq", split_axis=1, concat_axis=0, tiled=True),
        lax.all_to_all(values, "seq", split_axis=1, concat_axis=0, tiled=True),
    )
    width = head_acts.shape[1]
    klen = head_keys.shape[0]
    qlen = head_acts.shape[0]
    gain_row = lax.dynamic_slice_in_dim(gains[0], lax.axis_index("seq") * width, width, 0)
    query_all = (head_acts.astype(jnp.float32) * gain_row[None, :]).astype(jnp.bfloat16)
    positions = (offsets[:, None] + jnp.arange(tq_rows, dtype=jnp.int32)[None, :]).reshape(-1)
    key_heads = head_keys.reshape(klen, width // DH, DH)
    value_heads = head_values.reshape(klen, width // DH, DH)
    section_idx = lax.axis_index("section")
    acc_keys = jnp.zeros((klen, width), jnp.float32)
    acc_values = jnp.zeros((klen, width), jnp.float32)
    groups = 1
    group_rows = qlen // groups
    grad_all = jnp.zeros((qlen, width), jnp.bfloat16)
    incoming = jnp.zeros((group_rows, width), jnp.bfloat16)
    turns = groups + n_section - 1
    for turn in range(turns):
        group = turn - (n_section - 1 - section_idx)
        active = (group >= 0) & (group < groups)
        upstream = jnp.where(section_idx == n_section - 1, head_top, incoming)

        def run(operands):
            return layer_step(
                operands[0],
                operands[1],
                operands[2],
                gain_row,
                key_heads,
                value_heads,
                operands[3],
                operands[4],
            )

        def skip(operands):
            return (jnp.zeros((group_rows, width), jnp.bfloat16), operands[3], operands[4])

        grad_in, acc_keys, acc_values = lax.cond(
            active, run, skip, (query_all, upstream, positions, acc_keys, acc_values)
        )
        grad_all = jnp.where(active, grad_in, grad_all)
        if turn < turns - 1:
            incoming = passed_along(grad_in, "section", -1)
    sum_keys, sum_values = (
        lax.psum(acc_keys.astype(jnp.bfloat16), "section").astype(jnp.float32),
        lax.psum(acc_values.astype(jnp.bfloat16), "section").astype(jnp.float32),
    )
    round_keys = sum_keys.astype(jnp.bfloat16)
    round_values = sum_values.astype(jnp.bfloat16)
    out_acts, out_keys, out_values = (
        lax.all_to_all(grad_all, "seq", split_axis=0, concat_axis=1, tiled=True),
        lax.all_to_all(round_keys, "seq", split_axis=0, concat_axis=1, tiled=True),
        lax.all_to_all(round_values, "seq", split_axis=0, concat_axis=1, tiled=True),
    )
    return (out_acts[None], out_keys, out_values)


def solution(mesh):
    placed = (
        P("section", "seq", None),
        P("section", None),
        P("seq", None),
        P("seq", None),
        P("seq", None),
        P(),
    )
    return jax.shard_map(
        local,
        mesh=mesh,
        in_specs=placed,
        out_specs=(P("section", "seq", None), P("seq", None), P("seq", None)),
        check_vma=False,
    )
```

profile of v0, /device:TPU:1, one launch (start us, length us, event | category | flops | bytes accessed | tf_op | source)
XLA Modules:
  0.0 873.1 jit_solution(3839215287432362995)
XLA Ops:
  9.5 11.5 %all-to-all-start.2 = ((bf16[96,32,128]{2,0,1:T(8,128)(2,1)}), bf16[96,32,128]{2,0,1:T(8,128)(2,1)}, u32[]{:S(2)}, u32[]{:S(2)}) async-start(bf16[96,32,128]{2,0,1:T(8,128)(2,1)} %copy_bitcast_fusion.4), calls=%async_computation.2 | async-start | bytes 1572864 | tf_op jit(solution)/shard_map/all_to_all | solution.py:70
  23.1 11.1 %all-to-all-done.2 = bf16[96,32,128]{2,0,1:T(8,128)(2,1)} async-done(((bf16[96,32,128]{2,0,1:T(8,128)(2,1)}), bf16[96,32,128]{2,0,1:T(8,128)(2,1)}, u32[]{:S(2)}, u32[]{:S(2)}) %all-to-all-start.2) | async-done | bytes 786464 | tf_op jit(solution)/shard_map/all_to_all | solution.py:70
  34.2 5.8 all-to-all-start.3
  41.7 11.1 %all-to-all-done.3 = bf16[96,32,128]{2,0,1:T(8,128)(2,1)S(1)} async-done(((bf16[96,32,128]{2,0,1:T(8,128)(2,1)}), bf16[96,32,128]{2,0,1:T(8,128)(2,1)S(1)}, u32[]{:S(2)}, u32[]{:S(2)}) %all-to-all-start.3) | async-done | bytes 786464 | tf_op jit(solution)/shard_map/all_to_all | solution.py:71
  52.8 6.3 all-to-all-start.1
  60.5 14.0 %all-to-all-done.1 = bf16[128,32,128]{2,0,1:T(8,128)(2,1)S(1)} async-done(((bf16[128,32,128]{2,0,1:T(8,128)(2,1)}), bf16[128,32,128]{2,0,1:T(8,128)(2,1)S(1)}, u32[]{:S(2)}, u32[]{:S(2)}) %all-to-all-start.1) | async-done | bytes 1048608 | tf_op jit(solution)/shard_map/all_to_all | solution.py:68
  74.5 6.9 all-to-all-start
  83.4 13.4 %all-to-all-done = bf16[128,32,128]{2,0,1:T(8,128)(2,1)} async-done(((bf16[128,32,128]{2,0,1:T(8,128)(2,1)}), bf16[128,32,128]{2,0,1:T(8,128)(2,1)}, u32[]{:S(2)}, u32[]{:S(2)}) %all-to-all-start) | async-done | bytes 1048608 | tf_op jit(solution)/shard_map/all_to_all | solution.py:69
  97.0 3.8 conditional.4
  100.8 5.5 collective-permute-start
  106.3 13.0 %collective-permute-done = bf16[4096,128]{1,0:T(8,128)(2,1)S(1)} collective-permute-done((bf16[4096,128]{1,0:T(8,128)(2,1)}, bf16[4096,128]{1,0:T(8,128)(2,1)S(1)}, u32[]{:S(2)}, u32[]{:S(2)}) %collective-permute-start) | collective-permute-done | bytes 1048608 | tf_op jit(solution)/shard_map/ppermute | solution.py:12
  121.8 322.2 %collective-permute-done.1 = bf16[4096,128]{1,0:T(8,128)(2,1)S(1)} collective-permute-done((bf16[4096,128]{1,0:T(8,128)(2,1)S(1)}, bf16[4096,128]{1,0:T(8,128)(2,1)S(1)}, u32[]{:S(2)}, u32[]{:S(2)}) %collective-permute-start.1) | collective-permute-done | bytes 1048608 | tf_op jit(solution)/shard_map/ppermute | solution.py:12
  444.0 158.2 %conditional.6 = (bf16[4096,128]{1,0:T(8,128)(2,1)S(1)}, f32[3072,128]{0,1:T(8,128)}, f32[3072,128]{0,1:T(8,128)}) conditional(s32[]{:T(128)} %convert_element_type.91, (f32[3072,128]{0,1:T(8,128)}, f32[3072,128]{0,1:T(8,128)}) %tuple.60, (pred[]{:T(512)}, bf16[4096,128]{1,0:T(8,128)(2,1)}, bf16[4096,128]{1,0:T(8,128)(2,1)S(1)}, ...), branch_computations={%region_14.15_spmd, %region_15.21_spmd} | conditional | flops 2052848128 | bytes 83945752 | solution.py:109
  446.5 153.8 %while.54 = (s32[]{:T(128)}, f32[3072,128]{0,1:T(8,128)}, f32[3072,128]{0,1:T(8,128)}, f32[8,512,128]{2,1,0:T(8,128)}, bf16[8,512,128]{2,1,0:T(8,128)(2,1)}, /*i...) while((s32[]{:T(128)}, f32[3072,128]{0,1:T(8,128)}, ...), condition=%wide.region_20.20_spmd, body=%wide.region_16.19_spmd.sunk | while | flops 2050226688 | bytes 72377992 | solution.py:58
  459.2 3.3 fusion.185
  574.6 3.3 fusion.185
  593.8 3.3 fusion.185
  604.1 14.2 %collective-permute-done.2 = bf16[4096,128]{1,0:T(8,128)(2,1)S(1)} collective-permute-done((bf16[4096,128]{1,0:T(8,128)(2,1)S(1)}, bf16[4096,128]{1,0:T(8,128)(2,1)S(1)}, u32[]{:S(2)}, u32[]{:S(2)}) %collective-permute-start.2) | collective-permute-done | bytes 1048608 | tf_op jit(solution)/shard_map/ppermute | solution.py:12
  624.2 20.1 %all_to_all.118 = bf16[32,128,128]{2,1,0:T(8,128)(2,1)S(1)} all-to-all(bf16[32,128,128]{2,1,0:T(8,128)(2,1)S(1)} %bitcast.417), channel_id=1, replica_groups=mesh['section'=4,'seq'=32] {'seq'}, dimensions={0} | all-to-all | bytes 2097152 | tf_op jit(solution)/shard_map/all_to_all | solution.py:122
  644.3 179.1 %all-reduce.3.cloned.1.call-done = (bf16[32,96,128]{2,1,0:T(8,128)(2,1)}, bf16[32,96,128]{2,1,0:T(8,128)(2,1)}) async-done(((bf16[32,96,128]{2,1,0:T(8,128)(2,1)}, bf16[32,96,128]{2,1,0:T(8,128)(2,1)}), (bf16[32,96,128]{2,1,0:T(8,128)(2,1)}, bf16[32,96,128]{2,1,0:T(8,128)(2,1)})) %all-reduce.3.cloned.1.call-update) | async-done | bytes 1572880 | tf_op jit(solution)/shard_map/psum | solution.py:116
  823.4 9.2 %all-to-all-start.6 = ((bf16[32,96,128]{2,1,0:T(8,128)(2,1)}), bf16[32,96,128]{2,1,0:T(8,128)(2,1)}, u32[]{:S(2)}, u32[]{:S(2)}) async-start(bf16[32,96,128]{2,1,0:T(8,128)(2,1)} %get-tuple-element.469), calls=%async_computation.6 | async-start | bytes 1572864 | tf_op jit(solution)/shard_map/all_to_all | solution.py:124
  834.6 12.0 %all-to-all-done.6 = bf16[32,96,128]{2,1,0:T(8,128)(2,1)} async-done(((bf16[32,96,128]{2,1,0:T(8,128)(2,1)}), bf16[32,96,128]{2,1,0:T(8,128)(2,1)}, u32[]{:S(2)}, u32[]{:S(2)}) %all-to-all-start.6) | async-done | bytes 786464 | tf_op jit(solution)/shard_map/all_to_all | solution.py:124
  846.7 5.3 all-to-all-start.5
  854.0 11.1 %all-to-all-done.5 = bf16[32,96,128]{2,1,0:T(8,128)(2,1)S(1)} async-done(((bf16[32,96,128]{2,1,0:T(8,128)(2,1)}), bf16[32,96,128]{2,1,0:T(8,128)(2,1)S(1)}, u32[]{:S(2)}, u32[]{:S(2)}) %all-to-all-start.5) | async-done | bytes 786464 | tf_op jit(solution)/shard_map/all_to_all | solution.py:123
  (124 shorter events, 176.6 us)
Async XLA Ops:
  7.2 52.1 %copy-start = (bf16[128,4096]{1,0:T(8,128)(2,1)S(1)}, bf16[128,4096]{1,0:T(8,128)(2,1)}, u32[]{:S(2)}) copy-start(bf16[128,4096]{1,0:T(8,128)(2,1)} %param.24) | copy-start | bytes 3145732
  7.2 32.9 %copy-start.8 = (bf16[1,128,4096]{2,1,0:T(8,128)(2,1)S(1)}, bf16[1,128,4096]{2,1,0:T(8,128)(2,1)}, u32[]{:S(2)}) copy-start(bf16[1,128,4096]{2,1,0:T(8,128)(2,1)} %param.22) | copy-start | bytes 3145732
  7.2 51.9 %copy-start.17 = (s32[32]{0:T(128)S(1)}, s32[32]{0:T(128)}, u32[]{:S(2)}) copy-start(s32[32]{0:T(128)} %param.27) | copy-start | bytes 388
  9.5 24.7 %all-to-all-start.2 = ((bf16[96,32,128]{2,0,1:T(8,128)(2,1)}), bf16[96,32,128]{2,0,1:T(8,128)(2,1)}, u32[]{:S(2)}, u32[]{:S(2)}) async-start(bf16[96,32,128]{2,0,1:T(8,128)(2,1)} %copy_bitcast_fusion.4), calls=%async_computation.2 | async-start | bytes 1572864 | tf_op jit(solution)/shard_map/all_to_all | solution.py:70
  34.2 18.6 %all-to-all-start.3 = ((bf16[96,32,128]{2,0,1:T(8,128)(2,1)}), bf16[96,32,128]{2,0,1:T(8,128)(2,1)S(1)}, u32[]{:S(2)}, u32[]{:S(2)}) async-start(bf16[96,32,128]{2,0,1:T(8,128)(2,1)} %copy_bitcast_fusion.3), calls=%async_computation.3 | async-start | bytes 1572864 | tf_op jit(solution)/shard_map/all_to_all | solution.py:71
  52.8 44.1 %copy-start.11 = (bf16[96,32,128]{2,0,1:T(8,128)(2,1)}, bf16[96,32,128]{2,0,1:T(8,128)(2,1)S(1)}, u32[]{:S(2)}) copy-start(bf16[96,32,128]{2,0,1:T(8,128)(2,1)S(1)} %all-to-all-done.3) | copy-start | bytes 2359300
  52.8 21.7 %all-to-all-start.1 = ((bf16[128,32,128]{2,0,1:T(8,128)(2,1)}), bf16[128,32,128]{2,0,1:T(8,128)(2,1)S(1)}, u32[]{:S(2)}, u32[]{:S(2)}) async-start(bf16[128,32,128]{2,0,1:T(8,128)(2,1)} %copy.39), calls=%async_computation.1 | async-start | bytes 2097152 | tf_op jit(solution)/shard_map/all_to_all | solution.py:68
  74.5 22.3 %all-to-all-start = ((bf16[128,32,128]{2,0,1:T(8,128)(2,1)}), bf16[128,32,128]{2,0,1:T(8,128)(2,1)}, u32[]{:S(2)}, u32[]{:S(2)}) async-start(bf16[128,32,128]{2,0,1:T(8,128)(2,1)} %copy_bitcast_fusion), calls=%async_computation | async-start | bytes 2097152 | tf_op jit(solution)/shard_map/all_to_all | solution.py:69
  81.4 742.0 %all-reduce.3.cloned.1.call-start = ((), (), s32[]{:S(2)}) async-start(), calls=%async_computation.7 | async-start | bytes 3145728 | tf_op jit(solution)/shard_map/psum | solution.py:116
  100.8 18.5 %collective-permute-start = (bf16[4096,128]{1,0:T(8,128)(2,1)}, bf16[4096,128]{1,0:T(8,128)(2,1)S(1)}, u32[]{:S(2)}, u32[]{:S(2)}) collective-permute-start(bf16[4096,128]{1,0:T(8,128)(2,1)} %get-tuple-element.353), channel_id=1, source_target_pairs={{32,0},{64,32},{96,64},{33,1},{65,33},{97,65},{34,2},{66,34},{98,6... | collective-permute-start | bytes 3145736 | tf_op jit(solution)/shard_map/ppermute | solution.py:12
  119.8 324.2 %copy-start.6 = (bf16[4096,128]{1,0:T(8,128)(2,1)}, bf16[4096,128]{1,0:T(8,128)(2,1)S(1)}, u32[]{:S(2)}) copy-start(bf16[4096,128]{1,0:T(8,128)(2,1)S(1)} %get-tuple-element.356) | copy-start | bytes 3145732
  119.8 324.2 %collective-permute-start.1 = (bf16[4096,128]{1,0:T(8,128)(2,1)S(1)}, bf16[4096,128]{1,0:T(8,128)(2,1)S(1)}, u32[]{:S(2)}, u32[]{:S(2)}) collective-permute-start(bf16[4096,128]{1,0:T(8,128)(2,1)S(1)} %get-tuple-element.356), channel_id=1, source_target_pairs={{32,0},{64,32},{96,64},{33,1},{65,33},{97,65},{34,2},{66,34},{98,6... | collective-permute-start | bytes 3145736 | tf_op jit(solution)/shard_map/ppermute | solution.py:12
  446.5 4.9 copy-start.15
  465.8 4.9 copy-start.15
  485.0 4.9 copy-start.15
  504.2 4.9 copy-start.15
  523.5 4.9 copy-start.15
  542.7 4.9 copy-start.15
  561.9 4.9 copy-start.15
  602.2 16.1 %collective-permute-start.2 = (bf16[4096,128]{1,0:T(8,128)(2,1)S(1)}, bf16[4096,128]{1,0:T(8,128)(2,1)S(1)}, u32[]{:S(2)}, u32[]{:S(2)}) collective-permute-start(bf16[4096,128]{1,0:T(8,128)(2,1)S(1)} %get-tuple-element.359), channel_id=1, source_target_pairs={{32,0},{64,32},{96,64},{33,1},{65,33},{97,65},{34,2},{66,34},{98,6... | collective-permute-start | bytes 3145736 | tf_op jit(solution)/shard_map/ppermute | solution.py:12
  618.7 5.2 copy-start.7
  624.1 241.9 %copy-start.1 = (bf16[128,4096]{1,0:T(8,128)(2,1)S(1)}, bf16[128,4096]{1,0:T(8,128)(2,1)}, u32[]{:S(2)}) copy-start(bf16[128,4096]{1,0:T(8,128)(2,1)} %param.24) | copy-start | bytes 3145732
  823.4 23.2 %all-to-all-start.6 = ((bf16[32,96,128]{2,1,0:T(8,128)(2,1)}), bf16[32,96,128]{2,1,0:T(8,128)(2,1)}, u32[]{:S(2)}, u32[]{:S(2)}) async-start(bf16[32,96,128]{2,1,0:T(8,128)(2,1)} %get-tuple-element.469), calls=%async_computation.6 | async-start | bytes 1572864 | tf_op jit(solution)/shard_map/all_to_all | solution.py:124
  846.7 18.5 %all-to-all-start.5 = ((bf16[32,96,128]{2,1,0:T(8,128)(2,1)}), bf16[32,96,128]{2,1,0:T(8,128)(2,1)S(1)}, u32[]{:S(2)}, u32[]{:S(2)}) async-start(bf16[32,96,128]{2,1,0:T(8,128)(2,1)} %get-tuple-element.468), calls=%async_computation.5 | async-start | bytes 1572864 | tf_op jit(solution)/shard_map/all_to_all | solution.py:123
  (2 other events, 5.9 us)
Sparse Core Ops, SparseCore 0:
  624.1 199.3 all-reduce.2
where the time goes:
time: 885 us; the launch traced here: 873 us
  waiting for transfers between devices  601 us (68%)
  matrix products  121 us (14%)
  starting transfers between devices  54.3 us (6%)
  other arithmetic  37 us (4%)
  local copies, waits for them, and re-layouts  23.5 us (3%)
  blocking collectives  20.1 us (2%)
  between operations  14.5 us (2%)
    ppermute x3, waiting for transfers between devices, passed_along(): lax.ppermute(value, axis, [(source, source + steps) for source in range(i...  349 us
    psum x1, waiting for transfers between devices, local(): lax.psum(acc_keys.astype(jnp.bfloat16), 'section').astype(jnp.float32)  179 us
    dot_general x8, matrix products, block_grads(): jnp.einsum('hrk,rhd->khd', dscore, query_heads, preferred_element_type=jn...  26.7 us
    dot_general x8, matrix products, block_grads(): jnp.einsum('hrk,rhd->khd', probs_round, up_heads, preferred_element_type=...  25.5 us
    dot_general x8, matrix products, block_grads(): jnp.einsum('rhd,khd->hrk', up_heads, value_heads, preferred_element_type=...  25.5 us
    dot_general x8, matrix products, block_grads(): jnp.einsum('hrk,khd->rhd', dscore, key_heads, preferred_element_type=jnp....  22.6 us
    dot_general x8, matrix products, block_grads(): jnp.einsum('rhd,khd->hrk', query_heads, key_heads, preferred_element_type...  21 us
    all_to_all x1, blocking collectives, local(): lax.all_to_all(grad_all, 'seq', split_axis=0, concat_axis=1, tiled=True)  20.1 us
  transfers between devices with their start and end apart: 10, of which 10 were waited for; matrix products, arithmetic and copies ran while one was open for 1% of the time, Pallas kernels for 0%

commit v1 on v0

v1 whole, which is shorter than its diff:
```python
import jax
import jax.numpy as jnp
from jax import lax
from jax.experimental import pallas as pl
from jax.experimental.pallas import tpu as pltpu
from jax.sharding import PartitionSpec as P

DH = 128
SECT = 4
NB = 32
RB = 32
KLEN = 3072
TILE = 256
GRP = TILE // RB
CH = 1024
SCALE = 1.0 / DH**0.5
LOG2E = 1.4426950408889634
NT = (((1,), (1,)), ((), ()))
NN = (((1,), (0,)), ((), ()))


def fdot(a, b, dims=NN):
    return lax.dot_general(a, b, dims, preferred_element_type=jnp.float32)


def fold(x, op):
    return op(x.reshape(x.shape[0] // 8, 8, x.shape[1]), axis=0)


def compute_kernel(order, offs, q_in, top, keys, vals, gains, grad, dkv_out,
                   kt, sc, ex, dp, dk, dv, q_s, up_s, qn_s, un_s, dqt):
    first = lax.axis_index("section") * RB
    kt[...] = keys[...].T
    dk[...] = jnp.zeros_like(dk)
    dv[...] = jnp.zeros_like(dv)
    lane = lax.broadcasted_iota(jnp.int32, (1, TILE), 1)

    def tile_step(t, _):
        qpos = lax.rem(lane, RB) + first
        group = lax.div(lane, RB)
        for k in range(GRP):
            block = order[t * GRP + k]
            qpos = qpos + jnp.where(group == k, offs[block], 0)
            up_s[k * RB : (k + 1) * RB, :] = top[block]
        low = offs[order[t * GRP]] + first
        high = offs[order[t * GRP + GRP - 1]] + first + RB
        full = lax.div(low + 1, CH)
        total = lax.div(high + CH - 1, CH)

        def layer_step(turn, _):
            layer = SECT - 1 - turn
            gain = gains[layer][0:1, :]
            for k in range(GRP):
                block = order[t * GRP + k]
                q_s[k * RB : (k + 1) * RB, :] = (
                    q_in[layer, block].astype(jnp.float32) * gain
                ).astype(jnp.bfloat16)

            def scores(j, peak, masked):
                rows = pl.ds(pl.multiple_of(j * CH, CH), CH)
                s = fdot(keys[rows, :], q_s[...], NT)
                if masked:
                    spot = lax.broadcasted_iota(jnp.int32, (CH, TILE), 0) + j * CH
                    s = jnp.where(spot <= qpos, s, -1e30)
                sc[rows, :] = s
                return jnp.maximum(peak, fold(s, jnp.max))

            peak = jnp.full((8, TILE), -1e30, jnp.float32)
            peak = lax.fori_loop(0, full, lambda j, c: scores(j, c, False), peak)
            peak = lax.fori_loop(full, total, lambda j, c: scores(j, c, True), peak)
            peak = jnp.max(peak, axis=0, keepdims=True)

            def weights(j, carry):
                rows = pl.ds(pl.multiple_of(j * CH, CH), CH)
                e = jnp.exp2((sc[rows, :] - peak) * (SCALE * LOG2E))
                d = fdot(vals[rows, :], up_s[...], NT)
                ex[rows, :] = e.astype(jnp.bfloat16)
                dp[rows, :] = d
                return carry[0] + fold(e, jnp.sum), carry[1] + fold(e * d, jnp.sum)

            zero = jnp.zeros((8, TILE), jnp.float32)
            norm, delta = lax.fori_loop(0, total, weights, (zero, zero))
            inv = 1.0 / jnp.sum(norm, axis=0, keepdims=True)
            delta = jnp.sum(delta, axis=0, keepdims=True) * inv
            inv_rows = jnp.broadcast_to(inv, (DH, TILE)).T
            qn_s[...] = (q_s[...].astype(jnp.float32) * (inv_rows * SCALE)).astype(jnp.bfloat16)
            un_s[...] = (up_s[...].astype(jnp.float32) * inv_rows).astype(jnp.bfloat16)
            dqt[...] = jnp.zeros_like(dqt)

            def grads(j, _):
                rows = pl.ds(pl.multiple_of(j * CH, CH), CH)
                e = ex[rows, :]
                ds = (e.astype(jnp.float32) * (dp[rows, :] - delta)).astype(jnp.bfloat16)
                dqt[...] += fdot(kt[:, rows], ds)
                dk[rows, :] += fdot(ds, qn_s[...])
                dv[rows, :] += fdot(e, un_s[...])
                return 0

            lax.fori_loop(0, total, grads, 0)
            dq = (dqt[...] * (inv * SCALE)).T
            up = (up_s[...].astype(jnp.float32) + gain * dq).astype(jnp.bfloat16)
            up_s[...] = up
            for k in range(GRP):
                grad[layer, order[t * GRP + k]] = up[k * RB : (k + 1) * RB, :]
            return 0

        lax.fori_loop(0, SECT, layer_step, 0)
        return 0

    lax.fori_loop(0, NB * RB // TILE, tile_step, 0)
    dkv_out[0] = dk[...].astype(jnp.bfloat16)
    dkv_out[1] = dv[...].astype(jnp.bfloat16)


def compute(order, offs, q_in, top, keys, vals, gains):
    smem = pl.BlockSpec(memory_space=pltpu.SMEM)
    vmem = pl.BlockSpec(memory_space=pltpu.VMEM)
    return pl.pallas_call(
        compute_kernel,
        out_shape=(
            jax.ShapeDtypeStruct((SECT, NB, RB, DH), jnp.bfloat16),
            jax.ShapeDtypeStruct((2, KLEN, DH), jnp.bfloat16),
        ),
        in_specs=[smem, smem] + [vmem] * 5,
        out_specs=(vmem, vmem),
        scratch_shapes=[
            pltpu.VMEM((DH, KLEN), jnp.bfloat16),
            pltpu.VMEM((KLEN, TILE), jnp.float32),
            pltpu.VMEM((KLEN, TILE), jnp.bfloat16),
            pltpu.VMEM((KLEN, TILE), jnp.float32),
            pltpu.VMEM((KLEN, DH), jnp.float32),
            pltpu.VMEM((KLEN, DH), jnp.float32),
            pltpu.VMEM((TILE, DH), jnp.bfloat16),
            pltpu.VMEM((TILE, DH), jnp.bfloat16),
            pltpu.VMEM((TILE, DH), jnp.bfloat16),
            pltpu.VMEM((TILE, DH), jnp.bfloat16),
            pltpu.VMEM((DH, TILE), jnp.float32),
        ],
        compiler_params=pltpu.CompilerParams(vmem_limit_bytes=56 * 2**20),
    )(order, offs, q_in, top, keys, vals, gains)


SEQ = 32
HALF = 48
ALL = SECT * SEQ
MESH = pl.DeviceIdType.MESH


def greet(section, seq):
    barrier = pltpu.get_barrier_semaphore()
    me = section * SEQ + seq

    def hello(i, _):
        peer = lax.rem(me + i, ALL)
        pl.semaphore_signal(
            barrier, inc=1, device_id=(lax.div(peer, SEQ), lax.rem(peer, SEQ)), device_id_type=MESH
        )
        return 0

    lax.fori_loop(1, ALL, hello, 0)
    pl.semaphore_wait(barrier, ALL - 1)


def push(src, dst, send, recv, device):
    pltpu.make_async_remote_copy(
        src_ref=src, dst_ref=dst, send_sem=send, recv_sem=recv, device_id=device, device_id_type=MESH
    ).start()


def arrived(ref, sem):
    pltpu.make_async_copy(ref, ref, sem).wait()


def columns(head):
    return pl.ds(pl.multiple_of(head * DH, DH), DH)


def spread_kernel(acts, top, keys, vals, gain, q_out, top_out, k_out, v_out, g_out, send, recv):
    section, seq = lax.axis_index("section"), lax.axis_index("seq")
    core = lax.rem(section, 2)
    sibling = section + 1 - 2 * core
    greet(section, seq)

    def cached(i, _):
        head = lax.rem(seq + i, SEQ)
        push(keys.at[core, :, columns(head)], k_out.at[seq, core], send.at[0], recv.at[0], (section, head))
        push(vals.at[core, :, columns(head)], v_out.at[seq, core], send.at[1], recv.at[1], (section, head))
        return 0

    def queries(i, _):
        head = lax.rem(seq + i, SEQ)
        push(
            top.at[pl.ds(pl.multiple_of(section * RB, RB), RB), columns(head)],
            top_out.at[seq], send.at[2], recv.at[2], (section, head),
        )
        for j in range(SECT):
            group = lax.rem(section + j, SECT)
            push(
                acts.at[pl.ds(pl.multiple_of(group * RB, RB), RB), columns(head)],
                q_out.at[section * SEQ + seq], send.at[3], recv.at[3], (group, head),
            )
        return 0

    mine = pl.ds(pl.multiple_of(section * RB, RB), RB)
    pltpu.make_async_copy(keys.at[core, :, columns(seq)], k_out.at[seq, core], recv.at[0]).start()
    pltpu.make_async_copy(vals.at[core, :, columns(seq)], v_out.at[seq, core], recv.at[1]).start()
    pltpu.make_async_copy(top.at[mine, columns(seq)], top_out.at[seq], recv.at[2]).start()
    pltpu.make_async_copy(acts.at[mine, columns(seq)], q_out.at[section * SEQ + seq], recv.at[3]).start()
    pltpu.make_async_copy(gain, g_out.at[section], recv.at[4]).start()
    lax.fori_loop(1, SEQ, cached, 0)
    for j in range(1, SECT):
        group = lax.rem(section + j, SECT)
        push(gain, g_out.at[section], send.at[4], recv.at[4], (group, seq))
        push(
            acts.at[pl.ds(pl.multiple_of(group * RB, RB), RB), columns(seq)],
            q_out.at[section * SEQ + seq], send.at[3], recv.at[3], (group, seq),
        )
    lax.fori_loop(1, SEQ, queries, 0)
    arrived(k_out.at[:, core], recv.at[0])
    push(k_out.at[:, core], k_out.at[:, core], send.at[5], recv.at[5], (sibling, seq))
    arrived(v_out.at[:, core], recv.at[1])
    push(v_out.at[:, core], v_out.at[:, core], send.at[6], recv.at[6], (sibling, seq))
    arrived(top_out, recv.at[2])
    arrived(q_out, recv.at[3])
    arrived(g_out, recv.at[4])
    arrived(k_out.at[:, 1 - core], recv.at[5])
    arrived(v_out.at[:, 1 - core], recv.at[6])
    arrived(k_out.at[: SEQ - 1, core], send.at[0])
    arrived(v_out.at[: SEQ - 1, core], send.at[1])
    arrived(top_out.at[: SEQ - 1], send.at[2])
    arrived(q_out.at[: ALL - 1], send.at[3])
    arrived(g_out.at[: SECT - 1], send.at[4])
    arrived(k_out.at[:, core], send.at[5])
    arrived(v_out.at[:, core], send.at[6])


def spread(acts, top, keys, vals, gain):
    any_space = pl.BlockSpec(memory_space=pl.ANY)
    return pl.pallas_call(
        spread_kernel,
        out_shape=(
            jax.ShapeDtypeStruct((ALL, RB, DH), jnp.bfloat16),
            jax.ShapeDtypeStruct((SEQ, RB, DH), jnp.bfloat16),
            jax.ShapeDtypeStruct((SEQ, 2, HALF, DH), jnp.bfloat16),
            jax.ShapeDtypeStruct((SEQ, 2, HALF, DH), jnp.bfloat16),
            jax.ShapeDtypeStruct((SECT, 8, DH), jnp.float32),
        ),
        in_specs=[any_space] * 5,
        out_specs=(any_space,) * 5,
        scratch_shapes=[pltpu.SemaphoreType.DMA((7,)), pltpu.SemaphoreType.DMA((7,))],
        compiler_params=pltpu.CompilerParams(
            collective_id=0, has_side_effects=True, vmem_limit_bytes=56 * 2**20
        ),
    )(acts, top, keys, vals, gain)


def collect_kernel(grad, dkv, acts_out, kv_out, from_core, part, from_chip, total, send, recv):
    section, seq = lax.axis_index("section"), lax.axis_index("seq")
    core, chip = lax.rem(section, 2), lax.div(section, 2)
    sibling = section + 1 - 2 * core
    across = section + 2 - 4 * chip
    greet(section, seq)
    push(dkv.at[:, :, 1 - core], from_core, send.at[0], recv.at[0], (sibling, seq))
    mine = pl.ds(pl.multiple_of(section * RB, RB), RB)
    pltpu.make_async_copy(grad.at[section * SEQ + seq], acts_out.at[mine, columns(seq)], recv.at[1]).start()

    def rows_back(block, layer):
        push(
            grad.at[layer * SEQ + block], acts_out.at[mine, columns(seq)],
            send.at[1], recv.at[1], (layer, block),
        )

    def send_grads(i, _):
        block = lax.rem(seq + i, SEQ)
        for j in range(SECT):
            rows_back(block, lax.rem(section + j, SECT))
        return 0

    for j in range(1, SECT):
        rows_back(seq, lax.rem(section + j, SECT))
    lax.fori_loop(1, SEQ, send_grads, 0)

    arrived(from_core, recv.at[0])

    def add_core(i, _):
        for kv in range(2):
            part[kv, i] = (
                dkv[kv, i, core].astype(jnp.float32) + from_core[kv, i].astype(jnp.float32)
            ).astype(jnp.bfloat16)
        return 0

    lax.fori_loop(0, SEQ, add_core, 0)
    push(part.at[1 - chip], from_chip, send.at[2], recv.at[2], (across, seq))
    arrived(from_chip, recv.at[2])

    def add_chip(i, _):
        total[i] = (part[chip, i].astype(jnp.float32) + from_chip[i].astype(jnp.float32)).astype(jnp.bfloat16)
        return 0

    lax.fori_loop(0, SEQ, add_chip, 0)
    target = kv_out.at[chip, core, :, columns(seq)]
    pltpu.make_async_copy(total.at[seq], target, recv.at[3]).start()
    push(total.at[seq], target, send.at[3], recv.at[3], (across, seq))

    def send_totals(i, _):
        block = lax.rem(seq + i, SEQ)
        push(total.at[block], target, send.at[3], recv.at[3], (section, block))
        push(total.at[block], target, send.at[3], recv.at[3], (across, block))
        return 0

    lax.fori_loop(1, SEQ, send_totals, 0)
    arrived(kv_out.at[:, core], recv.at[3])
    push(kv_out.at[:, core], kv_out.at[:, core], send.at[4], recv.at[4], (sibling, seq))
    arrived(acts_out, recv.at[1])
    arrived(kv_out.at[:, 1 - core], recv.at[4])
    arrived(from_core, send.at[0])
    arrived(grad.at[: ALL - 1], send.at[1])
    arrived(from_chip, send.at[2])
    arrived(total, send.at[3])
    arrived(total.at[: SEQ - 1], send.at[3])
    arrived(kv_out.at[:, core], send.at[4])


def collect(grad, dkv):
    any_space = pl.BlockSpec(memory_space=pl.ANY)
    vmem = pl.BlockSpec(memory_space=pltpu.VMEM)
    return pl.pallas_call(
        collect_kernel,
        out_shape=(
            jax.ShapeDtypeStruct((SECT * RB, SEQ * DH), jnp.bfloat16),
            jax.ShapeDtypeStruct((2, 2, HALF, SEQ * DH), jnp.bfloat16),
        ),
        in_specs=[any_space, vmem],
        out_specs=(any_space, any_space),
        scratch_shapes=[
            pltpu.VMEM((2, SEQ, HALF, DH), jnp.bfloat16),
            pltpu.VMEM((2, SEQ, HALF, DH), jnp.bfloat16),
            pltpu.VMEM((SEQ, HALF, DH), jnp.bfloat16),
            pltpu.VMEM((SEQ, HALF, DH), jnp.bfloat16),
            pltpu.SemaphoreType.DMA((5,)),
            pltpu.SemaphoreType.DMA((5,)),
        ],
        compiler_params=pltpu.CompilerParams(
            collective_id=1, has_side_effects=True, vmem_limit_bytes=56 * 2**20
        ),
    )(grad, dkv)


def local(acts, gains, grad_top, keys, values, offsets):
    seq = lax.axis_index("seq")
    gain = jnp.broadcast_to(lax.dynamic_slice(gains, (0, seq * DH), (1, DH)), (8, DH))
    spot = jnp.arange(SEQ, dtype=jnp.int32)
    ahead = (offsets[None, :] < offsets[:, None]) | (
        (offsets[None, :] == offsets[:, None]) & (spot[None, :] < spot[:, None])
    )
    rank = jnp.sum(ahead.astype(jnp.int32), axis=1)
    order = jnp.sum(jnp.where(rank[None, :] == spot[:, None], spot[None, :], 0), axis=1)
    q_in, top, k_in, v_in, gain_all = spread(
        acts[0], grad_top, keys.reshape(2, HALF, -1), values.reshape(2, HALF, -1), gain
    )
    grad, dkv = compute(
        order, offsets, q_in.reshape(SECT, NB, RB, DH), top,
        k_in.reshape(KLEN, DH), v_in.reshape(KLEN, DH), gain_all,
    )
    out_acts, out_kv = collect(grad.reshape(ALL, RB, DH), dkv.reshape(2, SEQ, 2, HALF, DH))
    return (out_acts[None], out_kv[0].reshape(2 * HALF, -1), out_kv[1].reshape(2 * HALF, -1))


def solution(mesh):
    return jax.shard_map(
        local,
        mesh=mesh,
        in_specs=(
            P("section", "seq", None),
            P("section", None),
            P("seq", None),
            P("seq", None),
            P("seq", None),
            P(),
        ),
        out_specs=(P("section", "seq", None), P("seq", None), P("seq", None)),
        check_vma=False,
    )
```

time: 885 us -> 156 us (0.18); the launches traced: 873 us -> 155 us
  waiting for transfers between devices: 601 us -> 0 us
  Pallas kernels: 0 us -> 148 us
  matrix products: 121 us -> 0 us
  starting transfers between devices: 54.3 us -> 0 us
  other arithmetic: 37 us -> 1.55 us
  blocking collectives: 20.1 us -> 0 us
  local copies, waits for them, and re-layouts: 23.5 us -> 5.03 us
  between operations: 14.5 us -> 0.67 us
    ppermute x3 -> x0, waiting for transfers between devices: 349 us -> none  [passed_along(): lax.ppermute(value, axis, [(source, source + steps) for source in range(i...]
    psum x1 -> x0, waiting for transfers between devices: 179 us -> none  [local(): lax.psum(acc_keys.astype(jnp.bfloat16), 'section').astype(jnp.float32)]
    pallas_call x0 -> x3, Pallas kernels: none -> 148 us  [the longest x1 61.4 us: compute(): pl.pallas_call(compute_kernel, out_shape=(jax.ShapeDtypeStruct((SECT, NB,...]
    dot_general x40 -> x0, matrix products: 121 us -> none  [the longest x8 26.7 us: block_grads(): jnp.einsum('hrk,rhd->khd', dscore, query_heads, preferred_element_type=jn...]
    all_to_all x6 -> x0, waiting for transfers between devices: 72.8 us -> none  [the longest x1 14 us: local(): lax.all_to_all(acts[0], 'seq', split_axis=1, concat_axis=0, tiled=True)]
    all_to_all x6 -> x0, starting transfers between devices: 44.9 us -> none  [the longest x1 11.5 us: local(): lax.all_to_all(keys, 'seq', split_axis=1, concat_axis=0, tiled=True)]
    all_to_all x1 -> x0, blocking collectives: 20.1 us -> none  [local(): lax.all_to_all(grad_all, 'seq', split_axis=0, concat_axis=1, tiled=True)]
    convert_element_type x10 -> x0, other arithmetic: 17.6 us -> none  [the longest x8 14.5 us: block_grads(): dscore = (probs * (dprobs - delta) * scale).astype(jnp.bfloat16)]
  transfers between devices with their start and end apart: 10 -> 0, of which waited for: 10 -> 0; matrix products, arithmetic and copies ran while one was open for 1% -> 0% of each run, Pallas kernels for 0% -> 0%
where the time goes in v1:
time: 156 us; the launch traced here: 155 us
  Pallas kernels  148 us (95%)
  local copies, waits for them, and re-layouts  5.03 us (3%)
    pallas_call x1, Pallas kernels, compute(): pl.pallas_call(compute_kernel, out_shape=(jax.ShapeDtypeStruct((SECT, NB,...  61.4 us
    pallas_call x1, Pallas kernels, collect(): pl.pallas_call(collect_kernel, out_shape=(jax.ShapeDtypeStruct((SECT * RB...  45.9 us
    pallas_call x1, Pallas kernels, spread(): pl.pallas_call(spread_kernel, out_shape=(jax.ShapeDtypeStruct((ALL, RB, D...  40.7 us

profile of v1, /device:TPU:1, one launch (start us, length us, event | category | flops | bytes accessed | tf_op | source)
XLA Modules:
  0.0 155.2 jit_solution(9874677416828191473)
XLA Ops:
  0.6 0.0 copy-start
  0.6 0.7 copy-done
  1.4 0.9 convert_reduce_fusion
  2.3 0.6 select_reduce_fusion.order
  2.9 0.6 broadcast_in_dim.14.gain
  3.5 40.7 %shard_map.85 = (bf16[128,32,128]{2,1,0:T(8,128)(2,1)}, bf16[32,32,128]{2,1,0:T(8,128)(2,1)}, bf16[32,2,48,128]{3,2,1,0:T(8,128)(2,1)}, bf16[32,2,48,128]{3,2,1,0:T(8,128)(2,1)}, f32[4,8,128]{2,1,0:T(8,128)}) custom-call(bf16[128,4096]{1,0:T(8,128)(2,1)} %bitcast.17, bf16[128,4096]{1,0:T(8,128)(2,1)} %top.1, bf16[2,48,4096]{2,1,0:T(8,128)(2,1)} %bitcast.18, ...), custom_call_target="tpu_custom_call" | custom-call | tf_op jit(solution)/shard_map/pallas_call | solution.py:239
  44.2 61.4 %shard_map.86 = (bf16[4,32,32,128]{3,2,1,0:T(8,128)(2,1)}, bf16[2,3072,128]{2,1,0:T(8,128)(2,1)}) custom-call(s32[32]{0:T(128)} %select_reduce_fusion.order, s32[32]{0:T(128)} %offs.1, bf16[4,32,32,128]{3,2,1,0:T(8,128)(2,1)} %bitcast.15, bf16[32,32,128]{2,1,0:T(8,128)(2,1)} %get-tuple-element.13.top, bf16[3072,128]{1,0:T(8,128)(2,1)} %bitcast.22, ...), custom_call_target="tpu_custom_call" | custom-call | tf_op jit(solution)/shard_map/pallas_call | solution.py:118
  105.6 45.9 %shard_map.87 = (bf16[128,4096]{1,0:T(8,128)(2,1)}, bf16[2,2,48,4096]{3,2,1,0:T(8,128)(2,1)}) custom-call(bf16[128,32,128]{2,1,0:T(8,128)(2,1)} %bitcast.14, bf16[2,32,2,48,128]{4,3,2,1,0:T(8,128)(2,1)} %bitcast.13), custom_call_target="tpu_custom_call" | custom-call | tf_op jit(solution)/shard_map/pallas_call | solution.py:327
  151.5 0.0 copy-start.1
  151.5 2.7 %fusion.2 = (bf16[1,2,48,4096]{3,2,1,0:T(8,128)(2,1)}, bf16[1,2,48,4096]{3,2,1,0:T(8,128)(2,1)}) fusion(bf16[2,2,48,4096]{3,2,1,0:T(8,128)(2,1)} %get-tuple-element.20), kind=kLoop, calls=%fused_computation.7 | loop fusion | bytes 3145728 | tf_op jit(solution)/shard_map/slice | solution.py:366
  154.3 0.0 copy-done.1
  154.3 1.0 copy.10
  (1 shorter events, 0.0 us)
Async XLA Ops:
  0.6 0.7 copy-start
  151.5 2.8 %copy-start.1 = (bf16[128,4096]{1,0:T(8,128)(2,1)S(1)}, bf16[128,4096]{1,0:T(8,128)(2,1)}, u32[]{:S(2)}) copy-start(bf16[128,4096]{1,0:T(8,128)(2,1)} %get-tuple-element.19) | copy-start | bytes 3145732

commit v2 on v0

v2 whole, which is shorter than its diff:
```python
import jax
import jax.numpy as jnp
from jax import lax
from jax.experimental import pallas as pl
from jax.experimental.pallas import tpu as pltpu
from jax.sharding import PartitionSpec as P

DH = 128
SECT = 4
SEQ = 32
ALL = SECT * SEQ
RB = 32
HALF = 48
KHALF = SEQ * HALF
KLEN = 2 * KHALF
TILE = 256
GRP = TILE // RB
TILES = SEQ // GRP
STEPS = SECT * TILES
PIECES = 4
PBLOCKS = SEQ // PIECES
PROWS = PBLOCKS * HALF
SCALE = 1.0 / DH**0.5
LOG2E = 1.4426950408889634
NO_PEAK = -3e38
MESH = pl.DeviceIdType.MESH


def fdot(a, b):
    return lax.dot_general(a, b, (((1,), (0,)), ((), ())), preferred_element_type=jnp.float32)


def push(src, dst, send, recv, device):
    pltpu.make_async_remote_copy(
        src_ref=src, dst_ref=dst, send_sem=send, recv_sem=recv, device_id=device, device_id_type=MESH
    ).start()


def keep(src, dst, sem):
    pltpu.make_async_copy(src, dst, sem).start()


def arrived(ref, sem):
    pltpu.make_async_copy(ref, ref, sem).wait()


def columns(head):
    return pl.ds(pl.multiple_of(head * DH, DH), DH)


def rows_of(start, count):
    return pl.ds(pl.multiple_of(start, 16), count)


def fill_bias(offs, first, bias):
    sub = lax.broadcasted_iota(jnp.int32, (RB, 1), 0)
    wide = 512

    def tile_bias(t, _):
        def some(j, _):
            flat = lax.broadcasted_iota(jnp.int32, (1, wide), 1) + j * wide
            half = lax.div(flat, KHALF)
            inside = flat - half * KHALF
            spot = inside + lax.div(inside, HALF) * HALF + half * HALF
            cols = pl.ds(pl.multiple_of(j * wide, wide), wide)
            for k in range(GRP):
                qpos = sub + (first + offs[t * GRP + k])
                bias[t, k * RB : (k + 1) * RB, cols] = jnp.where(spot <= qpos, 0.0, -1e30)
            return 0

        lax.fori_loop(0, KLEN // wide, some, 0)
        return 0

    lax.fori_loop(0, TILES, tile_bias, 0)


def load_query(q_in, gains, step):
    layer, t = SECT - 1 - lax.div(step, TILES), lax.rem(step, TILES)
    q = q_in[pl.ds(layer * SEQ + t * GRP, GRP)].reshape(TILE, DH)
    return (q.astype(jnp.float32) * gains[layer][0:1, :]).astype(jnp.bfloat16)


def split_query(q):
    scaled = q.astype(jnp.float32) * (SCALE * LOG2E)
    high = scaled.astype(jnp.bfloat16)
    low = (scaled - high.astype(jnp.float32)).astype(jnp.bfloat16)
    return jnp.concatenate([high, low], axis=1)


def scores(t, slot, kk, q2_s, bias, sc):
    s = fdot(q2_s[...], kk[...]) + bias[t]
    sc[slot] = s
    peak = jnp.full((TILE, DH), NO_PEAK, jnp.float32)
    for c in range(KLEN // DH):
        peak = jnp.maximum(peak, s[:, c * DH : (c + 1) * DH])
    return peak


def one_step(step, peak, q_in, gains, k_in, grad, kk, vt, bias, sc, ex, dp, dkv, q2_s, up_s):
    layer, t = SECT - 1 - lax.div(step, TILES), lax.rem(step, TILES)
    after = jnp.minimum(step + 1, STEPS - 1)
    slot = lax.rem(step, 2)
    up_now = up_s[pl.ds(t * GRP, GRP)].reshape(TILE, DH)
    q2_s[...] = split_query(load_query(q_in, gains, after))
    norm = jnp.zeros((TILE, DH), jnp.float32)
    delta = jnp.zeros((TILE, DH), jnp.float32)
    d = fdot(up_now, vt[...])
    e = jnp.exp2(sc[slot] - peak)
    dp[...] = d
    ex[...] = e.astype(jnp.bfloat16)
    ed = e * d
    for c in range(KLEN // DH):
        norm = norm + e[:, c * DH : (c + 1) * DH]
        delta = delta + ed[:, c * DH : (c + 1) * DH]
    peak_after = scores(lax.rem(after, TILES), 1 - slot, kk, q2_s, bias, sc)
    inv = 1.0 / jnp.sum(norm, axis=1, keepdims=True)
    delta = jnp.sum(delta, axis=1, keepdims=True) * inv
    q = load_query(q_in, gains, step)
    qn = (q.astype(jnp.float32) * (inv * SCALE)).T.astype(jnp.bfloat16)
    un = (up_now.astype(jnp.float32) * inv).T.astype(jnp.bfloat16)
    e = ex[...]
    ds = e * (dp[...] - delta).astype(jnp.bfloat16)
    dq = fdot(ds, k_in[...])
    dkv[0] += fdot(qn, ds)
    dkv[1] += fdot(un, e)
    up = (up_now.astype(jnp.float32) + gains[layer][0:1, :] * (dq * (inv * SCALE))).astype(jnp.bfloat16)
    up = up.reshape(GRP, RB, DH)
    up_s[pl.ds(t * GRP, GRP)] = up
    grad[pl.ds(layer * SEQ + t * GRP, GRP)] = up
    return jnp.max(peak_after, axis=1, keepdims=True)


def fused_kernel(
    offs, acts, top, keys, vals, gain, acts_out, k_out, v_out,
    q_in, up_s, k_in, v_in, g_in, grad, kk, vt, bias, sc, ex, dp, dkv, q2_s,
    outgoing, from_core, part, from_chip, total, send, recv, ready,
):
    section, seq = lax.axis_index("section"), lax.axis_index("seq")
    core, chip = lax.rem(section, 2), lax.div(section, 2)
    sibling = section + 1 - 2 * core
    across = section + 2 - 4 * chip
    me = section * SEQ + seq
    mine = rows_of(section * RB, RB)

    barrier = pltpu.get_barrier_semaphore()

    def hello(i, _):
        pl.semaphore_signal(barrier, inc=1, device_id=(section, lax.rem(seq + i, SEQ)), device_id_type=MESH)
        return 0

    lax.fori_loop(1, SEQ, hello, 0)
    for j in range(1, SECT):
        pl.semaphore_signal(barrier, inc=1, device_id=(lax.rem(section + j, SECT), seq), device_id_type=MESH)
    fill_bias(offs, section * RB, bias)
    dkv[...] = jnp.zeros_like(dkv)
    pl.semaphore_wait(barrier, SEQ + SECT - 2)
    for j in range(1, SECT):
        pl.semaphore_signal(ready, inc=1, device_id=(lax.rem(section + j, SECT), seq), device_id_type=MESH)

    k_here = k_in.at[rows_of(core * KHALF + seq * HALF, HALF)]
    v_here = v_in.at[rows_of(core * KHALF + seq * HALF, HALF)]

    def send_cached(i, _):
        head = lax.rem(seq + i, SEQ)
        push(keys.at[core, :, columns(head)], k_here, send.at[0], recv.at[0], (section, head))
        push(vals.at[core, :, columns(head)], v_here, send.at[1], recv.at[1], (section, head))
        return 0

    def send_query(group, head):
        push(
            acts.at[rows_of(group * RB, RB), columns(head)], q_in.at[me],
            send.at[3], recv.at[3 + section], (group, head),
        )

    def send_queries():
        for j in range(1, SECT):
            send_query(lax.rem(section + j, SECT), seq)

        def some(i, _):
            for j in range(SECT):
                send_query(lax.rem(section + j, SECT), lax.rem(seq + i, SEQ))
            return 0

        lax.fori_loop(1, SEQ, some, 0)

    def send_top(i, _):
        head = lax.rem(seq + i, SEQ)
        push(top.at[mine, columns(head)], up_s.at[seq], send.at[2], recv.at[2], (section, head))
        return 0

    keep(keys.at[core, :, columns(seq)], k_here, recv.at[0])
    keep(vals.at[core, :, columns(seq)], v_here, recv.at[1])
    keep(top.at[mine, columns(seq)], up_s.at[seq], recv.at[2])
    keep(acts.at[mine, columns(seq)], q_in.at[me], recv.at[3 + section])
    keep(gain, g_in.at[section], recv.at[7])
    lax.fori_loop(1, SEQ, send_cached, 0)
    for j in range(1, SECT):
        push(gain, g_in.at[section], send.at[4], recv.at[7], (lax.rem(section + j, SECT), seq))
    pl.semaphore_wait(ready, SECT - 1)

    @pl.when(section == SECT - 1)
    def _():
        send_queries()

    lax.fori_loop(1, SEQ, send_top, 0)
    k_half, v_half = k_in.at[rows_of(core * KHALF, KHALF)], v_in.at[rows_of(core * KHALF, KHALF)]
    k_other, v_other = k_in.at[rows_of((1 - core) * KHALF, KHALF)], v_in.at[rows_of((1 - core) * KHALF, KHALF)]
    arrived(k_half, recv.at[0])
    push(k_half, k_half, send.at[5], recv.at[8], (sibling, seq))
    arrived(v_half, recv.at[1])
    push(v_half, v_half, send.at[6], recv.at[9], (sibling, seq))

    @pl.when(section != SECT - 1)
    def _():
        send_queries()

    arrived(k_other, recv.at[8])
    kt = k_in[...].T
    kk[:DH, :] = kt
    kk[DH:, :] = kt
    arrived(v_other, recv.at[9])
    vt[...] = v_in[...].T
    arrived(g_in, recv.at[7])
    arrived(q_in.at[pl.ds((SECT - 1) * SEQ, SEQ)], recv.at[3 + SECT - 1])
    q2_s[...] = split_query(load_query(q_in, g_in, 0))
    peak = jnp.max(scores(0, 0, kk, q2_s, bias, sc), axis=1, keepdims=True)
    arrived(up_s, recv.at[2])

    def attend(step, peak):
        layer, t = SECT - 1 - lax.div(step, TILES), lax.rem(step, TILES)

        @pl.when((t == TILES - 1) & (layer > 0))
        def _():
            arrived(q_in.at[pl.ds((layer - 1) * SEQ, SEQ)], recv.at[2 + layer])

        peak = one_step(step, peak, q_in, g_in, k_in, grad, kk, vt, bias, sc, ex, dp, dkv, q2_s, up_s)

        def send_grad(k, _):
            block = t * GRP + k
            own = (layer == section) & (block == seq)

            @pl.when(own)
            def _():
                keep(grad.at[layer * SEQ + block], acts_out.at[mine, columns(seq)], recv.at[10])

            @pl.when(jnp.logical_not(own))
            def _():
                push(
                    grad.at[layer * SEQ + block], acts_out.at[mine, columns(seq)],
                    send.at[7], recv.at[10], (layer, block),
                )

            return 0

        lax.fori_loop(0, GRP, send_grad, 0)
        return peak

    lax.fori_loop(0, STEPS, attend, peak)

    order = (1 - chip, chip)
    for turn in range(2):
        kv = order[turn]
        far = pl.ds(pl.multiple_of((1 - core) * KHALF, DH), KHALF)
        outgoing[turn] = dkv[kv, :, far].astype(jnp.bfloat16).T
        push(outgoing.at[turn], from_core.at[turn], send.at[8 + turn], recv.at[11 + turn], (sibling, seq))
    near = pl.ds(pl.multiple_of(core * KHALF, DH), KHALF)

    def piece_rows(p):
        return rows_of(lax.rem(lax.div(seq, PBLOCKS) + p, PIECES) * PROWS, PROWS)

    part[0] = dkv[order[0], :, near].T.astype(jnp.bfloat16)
    arrived(from_core.at[0], recv.at[11])
    for p in range(PIECES):
        rows = piece_rows(p)
        part[0, rows] = (part[0, rows].astype(jnp.float32) + from_core[0, rows].astype(jnp.float32)).astype(jnp.bfloat16)
        push(part.at[0, rows], from_chip.at[rows], send.at[10], recv.at[13 + p], (across, seq))
    part[1] = dkv[order[1], :, near].T.astype(jnp.bfloat16)
    arrived(from_core.at[1], recv.at[12])
    k_target = k_out.at[core, :, columns(seq)]
    v_target = v_out.at[core, :, columns(seq)]

    def send_totals(p, target, sem):
        start = lax.rem(lax.div(seq, PBLOCKS) + p, PIECES) * PBLOCKS

        def some(i, _):
            block = start + lax.rem(seq + i, PBLOCKS)
            src = total.at[rows_of(block * HALF, HALF)]

            @pl.when(block == seq)
            def _():
                keep(src, target, sem)

            @pl.when(block != seq)
            def _():
                push(src, target, send.at[11], sem, (section, block))

            push(src, target, send.at[11], sem, (across, block))
            return 0

        lax.fori_loop(0, PBLOCKS, some, 0)

    for p in range(PIECES):
        rows = piece_rows(p)
        arrived(from_chip.at[rows], recv.at[13 + p])
        total[rows] = (
            part[1, rows].astype(jnp.float32) + from_core[1, rows].astype(jnp.float32)
            + from_chip[rows].astype(jnp.float32)
        ).astype(jnp.bfloat16)

        @pl.when(chip == 0)
        def _():
            send_totals(p, k_target, recv.at[17])

        @pl.when(chip == 1)
        def _():
            send_totals(p, v_target, recv.at[20])

    arrived(k_out.at[core], recv.at[17])
    arrived(v_out.at[core], recv.at[20])
    push(k_out.at[core], k_out.at[core], send.at[12], recv.at[18], (sibling, seq))
    push(v_out.at[core], v_out.at[core], send.at[13], recv.at[19], (sibling, seq))
    arrived(acts_out, recv.at[10])
    arrived(k_out.at[1 - core], recv.at[18])
    arrived(v_out.at[1 - core], recv.at[19])

    arrived(k_in.at[: (SEQ - 1) * HALF], send.at[0])
    arrived(v_in.at[: (SEQ - 1) * HALF], send.at[1])
    arrived(up_s.at[: SEQ - 1], send.at[2])
    arrived(q_in.at[: ALL - 1], send.at[3])
    arrived(g_in.at[: SECT - 1], send.at[4])
    arrived(k_half, send.at[5])
    arrived(v_half, send.at[6])
    arrived(grad.at[: ALL - 1], send.at[7])
    arrived(outgoing.at[0], send.at[8])
    arrived(outgoing.at[1], send.at[9])
    arrived(from_chip, send.at[10])
    arrived(k_in.at[: (2 * SEQ - 1) * HALF], send.at[11])
    arrived(k_out.at[core], send.at[12])
    arrived(v_out.at[core], send.at[13])


def attention_grads(offs, acts, top, keys, vals, gain):
    bf = jnp.bfloat16
    any_space = pl.BlockSpec(memory_space=pl.ANY)
    return pl.pallas_call(
        fused_kernel,
        out_shape=(
            jax.ShapeDtypeStruct((SECT * RB, SEQ * DH), bf),
            jax.ShapeDtypeStruct((2, HALF, SEQ * DH), bf),
            jax.ShapeDtypeStruct((2, HALF, SEQ * DH), bf),
        ),
        in_specs=[pl.BlockSpec(memory_space=pltpu.SMEM)] + [any_space] * 5,
        out_specs=(any_space, any_space, any_space),
        scratch_shapes=[
            pltpu.VMEM((ALL, RB, DH), bf),
            pltpu.VMEM((SEQ, RB, DH), bf),
            pltpu.VMEM((KLEN, DH), bf),
            pltpu.VMEM((KLEN, DH), bf),
            pltpu.VMEM((SECT, 8, DH), jnp.float32),
            pltpu.VMEM((ALL, RB, DH), bf),
            pltpu.VMEM((2 * DH, KLEN), bf),
            pltpu.VMEM((DH, KLEN), bf),
            pltpu.VMEM((TILES, TILE, KLEN), jnp.float32),
            pltpu.VMEM((2, TILE, KLEN), jnp.float32),
            pltpu.VMEM((TILE, KLEN), bf),
            pltpu.VMEM((TILE, KLEN), jnp.float32),
            pltpu.VMEM((2, DH, KLEN), jnp.float32),
            pltpu.VMEM((TILE, 2 * DH), bf),
            pltpu.VMEM((2, KHALF, DH), bf),
            pltpu.VMEM((2, KHALF, DH), bf),
            pltpu.VMEM((2, KHALF, DH), bf),
            pltpu.VMEM((KHALF, DH), bf),
            pltpu.VMEM((KHALF, DH), bf),
            pltpu.SemaphoreType.DMA((14,)),
            pltpu.SemaphoreType.DMA((21,)),
            pltpu.SemaphoreType.REGULAR,
        ],
        compiler_params=pltpu.CompilerParams(
            collective_id=0, has_side_effects=True, vmem_limit_bytes=60 * 2**20
        ),
    )(offs, acts, top, keys, vals, gain)


def local(acts, gains, grad_top, keys, values, offsets):
    seq = lax.axis_index("seq")
    gain = jnp.broadcast_to(lax.dynamic_slice(gains, (0, seq * DH), (1, DH)), (8, DH))
    out_acts, out_keys, out_values = attention_grads(
        offsets, acts[0], grad_top, keys.reshape(2, HALF, -1), values.reshape(2, HALF, -1), gain
    )
    return (out_acts[None], out_keys.reshape(2 * HALF, -1), out_values.reshape(2 * HALF, -1))


def solution(mesh):
    return jax.shard_map(
        local,
        mesh=mesh,
        in_specs=(
            P("section", "seq", None),
            P("section", None),
            P("seq", None),
            P("seq", None),
            P("seq", None),
            P(),
        ),
        out_specs=(P("section", "seq", None), P("seq", None), P("seq", None)),
        check_vma=False,
    )
```

time: 885 us -> 111 us (0.13); the launches traced: 873 us -> 110 us
  waiting for transfers between devices: 601 us -> 0 us
  matrix products: 121 us -> 0 us
  Pallas kernels: 0 us -> 103 us
  starting transfers between devices: 54.3 us -> 0 us
  other arithmetic: 37 us -> 0 us
  blocking collectives: 20.1 us -> 0 us
  local copies, waits for them, and re-layouts: 23.5 us -> 5.97 us
  between operations: 14.5 us -> 0.66 us
    ppermute x3 -> x0, waiting for transfers between devices: 349 us -> none  [passed_along(): lax.ppermute(value, axis, [(source, source + steps) for source in range(i...]
    psum x1 -> x0, waiting for transfers between devices: 179 us -> none  [local(): lax.psum(acc_keys.astype(jnp.bfloat16), 'section').astype(jnp.float32)]
    dot_general x40 -> x0, matrix products: 121 us -> none  [the longest x8 26.7 us: block_grads(): jnp.einsum('hrk,rhd->khd', dscore, query_heads, preferred_element_type=jn...]
    pallas_call x0 -> x1, Pallas kernels: none -> 103 us  [attention_grads(): pl.pallas_call(fused_kernel, out_shape=(jax.ShapeDtypeStruct((SECT * RB,...]
    all_to_all x6 -> x0, waiting for transfers between devices: 72.8 us -> none  [the longest x1 14 us: local(): lax.all_to_all(acts[0], 'seq', split_axis=1, concat_axis=0, tiled=True)]
    all_to_all x6 -> x0, starting transfers between devices: 44.9 us -> none  [the longest x1 11.5 us: local(): lax.all_to_all(keys, 'seq', split_axis=1, concat_axis=0, tiled=True)]
    all_to_all x1 -> x0, blocking collectives: 20.1 us -> none  [local(): lax.all_to_all(grad_all, 'seq', split_axis=0, concat_axis=1, tiled=True)]
    reduce_sum x8 -> x0, other arithmetic: 17.8 us -> none  [block_grads(): probs = weights / jnp.sum(weights, axis=2, keepdims=True)]
  transfers between devices with their start and end apart: 10 -> 0, of which waited for: 10 -> 0; matrix products, arithmetic and copies ran while one was open for 1% -> 0% of each run, Pallas kernels for 0% -> 0%
where the time goes in v2:
time: 111 us; the launch traced here: 110 us
  Pallas kernels  103 us (93%)
  local copies, waits for them, and re-layouts  5.97 us (5%)
    pallas_call x1, Pallas kernels, attention_grads(): pl.pallas_call(fused_kernel, out_shape=(jax.ShapeDtypeStruct((SECT * RB,...  103 us
    unnamed x9, local copies, waits for them, and re-layouts  5.37 us

profile of v2, /device:TPU:1, one launch (start us, length us, event | category | flops | bytes accessed | tf_op | source)
XLA Modules:
  0.0 109.6 jit_solution(14321269605480837194)
XLA Ops:
  0.6 0.0 copy-start
  0.6 0.7 copy-done
  1.4 0.6 broadcast_in_dim.11.gain
  2.0 103.0 %shard_map.85 = (bf16[128,4096]{1,0:T(8,128)(2,1)}, bf16[2,48,4096]{2,1,0:T(8,128)(2,1)}, bf16[2,48,4096]{2,1,0:T(8,128)(2,1)}) custom-call(s32[32]{0:T(128)} %offs.1, bf16[128,4096]{1,0:T(8,128)(2,1)} %bitcast.8, bf16[128,4096]{1,0:T(8,128)(2,1)} %top.1, bf16[2,48,4096]{2,1,0:T(8,128)(2,1)} %bitcast.12, bf16[2,48,4096]{2,1,0:T(8,128)(2,1)} %bitcast.13, ...), custom_call_target="tpu_custom_call" | custom-call | tf_op jit(solution)/shard_map/pallas_call | solution.py:345
  104.9 0.0 copy-start.2
  105.0 2.4 %copy.12 = bf16[1,128,4096]{2,1,0:T(8,128)(2,1)} copy(bf16[1,128,4096]{2,1,0:T(8,128)(2,1)} %bitcast.9) | data formatting | bytes 2097152
  107.3 0.0 copy-done.2
  107.3 0.0 copy-start.1
  107.3 0.9 copy.13
  108.2 0.5 copy-done.1
  108.7 0.9 copy.14
  (1 shorter events, 0.0 us)
Async XLA Ops:
  0.6 0.7 copy-start
  104.9 2.4 %copy-start.2 = (bf16[2,48,4096]{2,1,0:T(8,128)(2,1)S(1)}, bf16[2,48,4096]{2,1,0:T(8,128)(2,1)}, u32[]{:S(2)}) copy-start(bf16[2,48,4096]{2,1,0:T(8,128)(2,1)} %get-tuple-element.7) | copy-start | bytes 2359300
  107.3 1.4 %copy-start.1 = (bf16[2,48,4096]{2,1,0:T(8,128)(2,1)S(1)}, bf16[2,48,4096]{2,1,0:T(8,128)(2,1)}, u32[]{:S(2)}) copy-start(bf16[2,48,4096]{2,1,0:T(8,128)(2,1)} %get-tuple-element.8) | copy-start | bytes 2359300

commit v3 on v2

--- a/solution.py
+++ b/solution.py
@@ -17,8 +17,8 @@
 GRP = TILE // RB
 TILES = SEQ // GRP
 STEPS = SECT * TILES
-PIECES = 4
-PBLOCKS = SEQ // PIECES
+SIDE = KHALF // 2
+PBLOCKS = 8
 PROWS = PBLOCKS * HALF
 SCALE = 1.0 / DH**0.5
 LOG2E = 1.4426950408889634
@@ -52,6 +52,23 @@
     return pl.ds(pl.multiple_of(start, 16), count)
 
 
+def side_of(z):
+    return lax.rem(lax.div(z + 1, 2), 2)
+
+
+def block_at(y, which, side):
+    x, later = lax.div(which, 2), lax.rem(which, 2)
+    return (x * 2 + y) * 4 + side + later * (3 - 2 * side)
+
+
+def head_at(section, seq):
+    return lax.div(seq, 4) * 4 + lax.div(section, 2) * 2 + lax.div(lax.rem(seq, 4), 2)
+
+
+def group_at(section, seq):
+    return lax.rem(seq, 2) * 2 + lax.rem(section, 2)
+
+
 def fill_bias(offs, first, bias):
     sub = lax.broadcasted_iota(jnp.int32, (RB, 1), 0)
     wide = 512
@@ -59,9 +76,11 @@
     def tile_bias(t, _):
         def some(j, _):
             flat = lax.broadcasted_iota(jnp.int32, (1, wide), 1) + j * wide
-            half = lax.div(flat, KHALF)
-            inside = flat - half * KHALF
-            spot = inside + lax.div(inside, HALF) * HALF + half * HALF
+            half, side = lax.div(flat, KHALF), lax.rem(lax.div(flat, SIDE), 2)
+            inside = lax.rem(flat, SIDE)
+            which = lax.div(inside, HALF)
+            block = block_at(lax.div(which, 8), lax.rem(which, 8), side)
+            spot = block * (2 * HALF) + half * HALF + lax.rem(inside, HALF)
             cols = pl.ds(pl.multiple_of(j * wide, wide), wide)
             for k in range(GRP):
                 qpos = sub + (first + offs[t * GRP + k])
@@ -140,7 +159,11 @@
     sibling = section + 1 - 2 * core
     across = section + 2 - 4 * chip
     me = section * SEQ + seq
-    mine = rows_of(section * RB, RB)
+    head, group = head_at(section, seq), group_at(section, seq)
+    partner = seq + 1 - 2 * lax.rem(seq, 2)
+    x, y, z = lax.div(seq, 8), lax.rem(lax.div(seq, 4), 2), lax.rem(seq, 4)
+    side = side_of(z)
+    mine = rows_of(group * RB, RB)
 
     barrier = pltpu.get_barrier_semaphore()
 
@@ -151,26 +174,27 @@
     lax.fori_loop(1, SEQ, hello, 0)
     for j in range(1, SECT):
         pl.semaphore_signal(barrier, inc=1, device_id=(lax.rem(section + j, SECT), seq), device_id_type=MESH)
-    fill_bias(offs, section * RB, bias)
+    fill_bias(offs, group * RB, bias)
     dkv[...] = jnp.zeros_like(dkv)
     pl.semaphore_wait(barrier, SEQ + SECT - 2)
     for j in range(1, SECT):
         pl.semaphore_signal(ready, inc=1, device_id=(lax.rem(section + j, SECT), seq), device_id_type=MESH)
 
-    k_here = k_in.at[rows_of(core * KHALF + seq * HALF, HALF)]
-    v_here = v_in.at[rows_of(core * KHALF + seq * HALF, HALF)]
+    here = rows_of(core * KHALF + side * SIDE + (y * 8 + x * 2 + lax.div(z, 2)) * HALF, HALF)
+    k_here, v_here = k_in.at[here], v_in.at[here]
 
     def send_cached(i, _):
-        head = lax.rem(seq + i, SEQ)
-        push(keys.at[core, :, columns(head)], k_here, send.at[0], recv.at[0], (section, head))
-        push(vals.at[core, :, columns(head)], v_here, send.at[1], recv.at[1], (section, head))
+        to = lax.rem(seq + i, SEQ)
+        there = head_at(section, to)
+        push(keys.at[core, :, columns(there)], k_here, send.at[0], recv.at[0], (section, to))
+        push(vals.at[core, :, columns(there)], v_here, send.at[1], recv.at[1], (section, to))
         return 0
 
-    def send_query(group, head):
-        push(
-            acts.at[rows_of(group * RB, RB), columns(head)], q_in.at[me],
-            send.at[3], recv.at[3 + section], (group, head),
-        )
+    def query_rows(to_section, to):
+        return acts.at[rows_of(group_at(to_section, to) * RB, RB), columns(head_at(to_section, to))]
+
+    def send_query(to_section, to):
+        push(query_rows(to_section, to), q_in.at[me], send.at[3], recv.at[3 + section], (to_section, to))
 
     def send_queries():
         for j in range(1, SECT):
@@ -183,25 +207,29 @@
 
         lax.fori_loop(1, SEQ, some, 0)
 
+    def top_rows(to):
+        return top.at[rows_of(group_at(section, to) * RB, RB), columns(head_at(section, to))]
+
     def send_top(i, _):
-        head = lax.rem(seq + i, SEQ)
-        push(top.at[mine, columns(head)], up_s.at[seq], send.at[2], recv.at[2], (section, head))
+        to = lax.rem(seq + i, SEQ)
+        push(top_rows(to), up_s.at[seq], send.at[2], recv.at[2], (section, to))
         return 0
 
-    keep(keys.at[core, :, columns(seq)], k_here, recv.at[0])
-    keep(vals.at[core, :, columns(seq)], v_here, recv.at[1])
-    keep(top.at[mine, columns(seq)], up_s.at[seq], recv.at[2])
-    keep(acts.at[mine, columns(seq)], q_in.at[me], recv.at[3 + section])
-    keep(gain, g_in.at[section], recv.at[7])
-    lax.fori_loop(1, SEQ, send_cached, 0)
-    for j in range(1, SECT):
-        push(gain, g_in.at[section], send.at[4], recv.at[7], (lax.rem(section + j, SECT), seq))
+    keep(keys.at[core, :, columns(head)], k_here, recv.at[0])
+    keep(vals.at[core, :, columns(head)], v_here, recv.at[1])
+    keep(top_rows(seq), up_s.at[seq], recv.at[2])
+    keep(query_rows(section, seq), q_in.at[me], recv.at[3 + section])
+    keep(gain.at[chip], g_in.at[section], recv.at[7])
     pl.semaphore_wait(ready, SECT - 1)
 
     @pl.when(section == SECT - 1)
     def _():
         send_queries()
 
+    lax.fori_loop(1, SEQ, send_cached, 0)
+    for j in range(1, SECT):
+        to_section = lax.rem(section + j, SECT)
+        push(gain.at[lax.div(to_section, 2)], g_in.at[section], send.at[4], recv.at[7], (to_section, seq))
     lax.fori_loop(1, SEQ, send_top, 0)
     k_half, v_half = k_in.at[rows_of(core * KHALF, KHALF)], v_in.at[rows_of(core * KHALF, KHALF)]
     k_other, v_other = k_in.at[rows_of((1 - core) * KHALF, KHALF)], v_in.at[rows_of((1 - core) * KHALF, KHALF)]
@@ -241,12 +269,12 @@
 
             @pl.when(own)
             def _():
-                keep(grad.at[layer * SEQ + block], acts_out.at[mine, columns(seq)], recv.at[10])
+                keep(grad.at[layer * SEQ + block], acts_out.at[mine, columns(head)], recv.at[10])
 
             @pl.when(jnp.logical_not(own))
             def _():
                 push(
-                    grad.at[layer * SEQ + block], acts_out.at[mine, columns(seq)],
+                    grad.at[layer * SEQ + block], acts_out.at[mine, columns(head)],
                     send.at[7], recv.at[10], (layer, block),
                 )
 
@@ -257,71 +285,63 @@
 
     lax.fori_loop(0, STEPS, attend, peak)
 
-    order = (1 - chip, chip)
-    for turn in range(2):
-        kv = order[turn]
-        far = pl.ds(pl.multiple_of((1 - core) * KHALF, DH), KHALF)
-        outgoing[turn] = dkv[kv, :, far].astype(jnp.bfloat16).T
-        push(outgoing.at[turn], from_core.at[turn], send.at[8 + turn], recv.at[11 + turn], (sibling, seq))
-    near = pl.ds(pl.multiple_of(core * KHALF, DH), KHALF)
-
-    def piece_rows(p):
-        return rows_of(lax.rem(lax.div(seq, PBLOCKS) + p, PIECES) * PROWS, PROWS)
-
-    part[0] = dkv[order[0], :, near].T.astype(jnp.bfloat16)
-    arrived(from_core.at[0], recv.at[11])
-    for p in range(PIECES):
-        rows = piece_rows(p)
-        part[0, rows] = (part[0, rows].astype(jnp.float32) + from_core[0, rows].astype(jnp.float32)).astype(jnp.bfloat16)
-        push(part.at[0, rows], from_chip.at[rows], send.at[10], recv.at[13 + p], (across, seq))
-    part[1] = dkv[order[1], :, near].T.astype(jnp.bfloat16)
-    arrived(from_core.at[1], recv.at[12])
-    k_target = k_out.at[core, :, columns(seq)]
-    v_target = v_out.at[core, :, columns(seq)]
-
-    def send_totals(p, target, sem):
-        start = lax.rem(lax.div(seq, PBLOCKS) + p, PIECES) * PBLOCKS
-
+    near_half = pl.ds(pl.multiple_of(core * KHALF, DH), KHALF)
+    far_half = pl.ds(pl.multiple_of((1 - core) * KHALF, DH), KHALF)
+    for kv in range(2):
+        outgoing[kv] = dkv[kv, :, far_half].astype(jnp.bfloat16).T
+        push(outgoing.at[kv], from_core.at[kv], send.at[8 + kv], recv.at[11 + kv], (sibling, seq))
+
+    def add_core(kv, rows):
+        return part[kv, rows].astype(jnp.float32) + from_core[kv, rows].astype(jnp.float32)
+
+    def piece(p):
+        return lax.rem(y + p, 2) * PROWS
+
+    for kv in range(2):
+        part[kv] = dkv[kv, :, near_half].astype(jnp.bfloat16).T
+        arrived(from_core.at[kv], recv.at[11 + kv])
+        for p in range(2):
+            rows = rows_of((1 - side) * SIDE + piece(p), PROWS)
+            part[kv, rows] = add_core(kv, rows).astype(jnp.bfloat16)
+            push(
+                part.at[kv, rows], from_chip.at[kv, rows_of(piece(p), PROWS)],
+                send.at[10], recv.at[13 + 2 * kv + p], (section, partner),
+            )
+
+    def send_totals(kv, p, target):
         def some(i, _):
-            block = start + lax.rem(seq + i, PBLOCKS)
-            src = total.at[rows_of(block * HALF, HALF)]
+            which = lax.rem(2 * x + i, PBLOCKS)
+            block = block_at(lax.rem(y + p, 2), which, side)
+            src = total.at[kv, rows_of(piece(p) + which * HALF, HALF)]
 
             @pl.when(block == seq)
             def _():
-                keep(src, target, sem)
+                keep(src, target, recv.at[17 + kv])
 
             @pl.when(block != seq)
             def _():
-                push(src, target, send.at[11], sem, (section, block))
-
-            push(src, target, send.at[11], sem, (across, block))
+                push(src, target, send.at[11 + kv], recv.at[17 + kv], (section, block))
+
+            push(src, target, send.at[11 + kv], recv.at[17 + kv], (across, block))
             return 0
 
         lax.fori_loop(0, PBLOCKS, some, 0)
 
-    for p in range(PIECES):
-        rows = piece_rows(p)
-        arrived(from_chip.at[rows], recv.at[13 + p])
-        total[rows] = (
-            part[1, rows].astype(jnp.float32) + from_core[1, rows].astype(jnp.float32)
-            + from_chip[rows].astype(jnp.float32)
-        ).astype(jnp.bfloat16)
-
-        @pl.when(chip == 0)
-        def _():
-            send_totals(p, k_target, recv.at[17])
-
-        @pl.when(chip == 1)
-        def _():
-            send_totals(p, v_target, recv.at[20])
-
-    arrived(k_out.at[core], recv.at[17])
-    arrived(v_out.at[core], recv.at[20])
-    push(k_out.at[core], k_out.at[core], send.at[12], recv.at[18], (sibling, seq))
-    push(v_out.at[core], v_out.at[core], send.at[13], recv.at[19], (sibling, seq))
+    for kv, out in ((0, k_out), (1, v_out)):
+        for p in range(2):
+            done = rows_of(piece(p), PROWS)
+            arrived(from_chip.at[kv, done], recv.at[13 + 2 * kv + p])
+            total[kv, done] = (
+                add_core(kv, rows_of(side * SIDE + piece(p), PROWS)) + from_chip[kv, done].astype(jnp.float32)
+            ).astype(jnp.bfloat16)
+            send_totals(kv, p, out.at[core, :, columns(head)])
+
+    for kv, out in ((0, k_out), (1, v_out)):
+        arrived(out.at[core], recv.at[17 + kv])
+        push(out.at[core], out.at[core], send.at[13 + kv], recv.at[19 + kv], (sibling, seq))
     arrived(acts_out, recv.at[10])
-    arrived(k_out.at[1 - core], recv.at[18])
-    arrived(v_out.at[1 - core], recv.at[19])
+    for kv, out in ((0, k_out), (1, v_out)):
+        arrived(out.at[1 - core], recv.at[19 + kv])
 
     arrived(k_in.at[: (SEQ - 1) * HALF], send.at[0])
     arrived(v_in.at[: (SEQ - 1) * HALF], send.at[1])
@@ -331,12 +351,11 @@
     arrived(k_half, send.at[5])
     arrived(v_half, send.at[6])
     arrived(grad.at[: ALL - 1], send.at[7])
-    arrived(outgoing.at[0], send.at[8])
-    arrived(outgoing.at[1], send.at[9])
     arrived(from_chip, send.at[10])
-    arrived(k_in.at[: (2 * SEQ - 1) * HALF], send.at[11])
-    arrived(k_out.at[core], send.at[12])
-    arrived(v_out.at[core], send.at[13])
+    for kv, out in ((0, k_out), (1, v_out)):
+        arrived(outgoing.at[kv], send.at[8 + kv])
+        arrived(k_in.at[: (SEQ - 1) * HALF], send.at[11 + kv])
+        arrived(out.at[core], send.at[13 + kv])
 
 
 def attention_grads(offs, acts, top, keys, vals, gain):
@@ -369,9 +388,9 @@
             pltpu.VMEM((2, KHALF, DH), bf),
             pltpu.VMEM((2, KHALF, DH), bf),
             pltpu.VMEM((2, KHALF, DH), bf),
-            pltpu.VMEM((KHALF, DH), bf),
-            pltpu.VMEM((KHALF, DH), bf),
-            pltpu.SemaphoreType.DMA((14,)),
+            pltpu.VMEM((2, SIDE, DH), bf),
+            pltpu.VMEM((2, SIDE, DH), bf),
+            pltpu.SemaphoreType.DMA((15,)),
             pltpu.SemaphoreType.DMA((21,)),
             pltpu.SemaphoreType.REGULAR,
         ],
@@ -382,8 +401,9 @@
 
 
 def local(acts, gains, grad_top, keys, values, offsets):
-    seq = lax.axis_index("seq")
-    gain = jnp.broadcast_to(lax.dynamic_slice(gains, (0, seq * DH), (1, DH)), (8, DH))
+    low_head = head_at(0, lax.axis_index("seq"))
+    slices = [lax.dynamic_slice(gains, (0, (low_head + step) * DH), (1, DH)) for step in (0, 2)]
+    gain = jnp.broadcast_to(jnp.stack(slices), (2, 8, DH))
     out_acts, out_keys, out_values = attention_grads(
         offsets, acts[0], grad_top, keys.reshape(2, HALF, -1), values.reshape(2, HALF, -1), gain
     )

time: 111 us -> 106 us (0.955)
  Pallas kernels: 103 us -> 98.7 us
    pallas_call x1, Pallas kernels: 103 us -> 98.7 us  [attention_grads(): pl.pallas_call(fused_kernel, out_shape=(jax.ShapeDtypeStruct((SECT * RB,...]
    unnamed x9 -> x7, local copies, waits for them, and re-layouts: 5.37 us -> 4.66 us
where the time goes in v3:
time: 106 us; the launch traced here: 105 us
  Pallas kernels  98.7 us (93%)
  local copies, waits for them, and re-layouts  5.94 us (6%)
    pallas_call x1, Pallas kernels, attention_grads(): pl.pallas_call(fused_kernel, out_shape=(jax.ShapeDtypeStruct((SECT * RB,...  98.7 us
    unnamed x7, local copies, waits for them, and re-layouts  4.66 us

profile of v3, /device:TPU:1, one launch (start us, length us, event | category | flops | bytes accessed | tf_op | source)
XLA Modules:
  0.0 105.3 jit_solution(2832262023321934912)
XLA Ops:
  0.7 0.7 dynamic-slice_bitcast_fusion.1
  1.3 0.6 broadcast_in_dim.11.gain
  1.9 98.7 %shard_map.85 = (bf16[128,4096]{1,0:T(8,128)(2,1)}, bf16[2,48,4096]{2,1,0:T(8,128)(2,1)}, bf16[2,48,4096]{2,1,0:T(8,128)(2,1)}) custom-call(s32[32]{0:T(128)} %offs.1, bf16[128,4096]{1,0:T(8,128)(2,1)} %bitcast.12, bf16[128,4096]{1,0:T(8,128)(2,1)} %top.1, bf16[2,48,4096]{2,1,0:T(8,128)(2,1)} %bitcast.15, bf16[2,48,4096]{2,1,0:T(8,128)(2,1)} %bitcast.16, ...), custom_call_target="tpu_custom_call" | custom-call | tf_op jit(solution)/shard_map/pallas_call | solution.py:364
  100.7 0.0 copy-start.1
  100.7 2.4 %copy.12 = bf16[1,128,4096]{2,1,0:T(8,128)(2,1)} copy(bf16[1,128,4096]{2,1,0:T(8,128)(2,1)} %bitcast.11) | data formatting | bytes 2097152
  103.0 0.0 copy-done.1
  103.0 0.0 copy-start
  103.0 0.9 copy.13
  103.9 0.5 copy-done
  104.4 0.9 copy.14
  (1 shorter events, 0.0 us)
Async XLA Ops:
  100.7 2.4 %copy-start.1 = (bf16[2,48,4096]{2,1,0:T(8,128)(2,1)S(1)}, bf16[2,48,4096]{2,1,0:T(8,128)(2,1)}, u32[]{:S(2)}) copy-start(bf16[2,48,4096]{2,1,0:T(8,128)(2,1)} %get-tuple-element.7) | copy-start | bytes 2359300
  103.0 1.4 %copy-start = (bf16[2,48,4096]{2,1,0:T(8,128)(2,1)S(1)}, bf16[2,48,4096]{2,1,0:T(8,128)(2,1)}, u32[]{:S(2)}) copy-start(bf16[2,48,4096]{2,1,0:T(8,128)(2,1)} %get-tuple-element.8) | copy-start | bytes 2359300

commit v4 on v3

--- a/solution.py
+++ b/solution.py
@@ -93,8 +93,12 @@
     lax.fori_loop(0, TILES, tile_bias, 0)
 
 
-def load_query(q_in, gains, step):
-    layer, t = SECT - 1 - lax.div(step, TILES), lax.rem(step, TILES)
+def at_step(step, turn):
+    return SECT - 1 - lax.div(step, TILES), lax.rem(step + turn, TILES)
+
+
+def load_query(q_in, gains, step, turn):
+    layer, t = at_step(step, turn)
     q = q_in[pl.ds(layer * SEQ + t * GRP, GRP)].reshape(TILE, DH)
     return (q.astype(jnp.float32) * gains[layer][0:1, :]).astype(jnp.bfloat16)
 
@@ -115,12 +119,12 @@
     return peak
 
 
-def one_step(step, peak, q_in, gains, k_in, grad, kk, vt, bias, sc, ex, dp, dkv, q2_s, up_s):
-    layer, t = SECT - 1 - lax.div(step, TILES), lax.rem(step, TILES)
+def one_step(step, turn, peak, q_in, gains, k_in, grad, kk, vt, bias, sc, ex, dp, dkv, q2_s, up_s):
+    layer, t = at_step(step, turn)
     after = jnp.minimum(step + 1, STEPS - 1)
     slot = lax.rem(step, 2)
     up_now = up_s[pl.ds(t * GRP, GRP)].reshape(TILE, DH)
-    q2_s[...] = split_query(load_query(q_in, gains, after))
+    q2_s[...] = split_query(load_query(q_in, gains, after, turn))
     norm = jnp.zeros((TILE, DH), jnp.float32)
     delta = jnp.zeros((TILE, DH), jnp.float32)
     d = fdot(up_now, vt[...])
@@ -131,10 +135,10 @@
     for c in range(KLEN // DH):
         norm = norm + e[:, c * DH : (c + 1) * DH]
         delta = delta + ed[:, c * DH : (c + 1) * DH]
-    peak_after = scores(lax.rem(after, TILES), 1 - slot, kk, q2_s, bias, sc)
+    peak_after = scores(at_step(after, turn)[1], 1 - slot, kk, q2_s, bias, sc)
     inv = 1.0 / jnp.sum(norm, axis=1, keepdims=True)
     delta = jnp.sum(delta, axis=1, keepdims=True) * inv
-    q = load_query(q_in, gains, step)
+    q = load_query(q_in, gains, step, turn)
     qn = (q.astype(jnp.float32) * (inv * SCALE)).T.astype(jnp.bfloat16)
     un = (up_now.astype(jnp.float32) * inv).T.astype(jnp.bfloat16)
     e = ex[...]
@@ -150,9 +154,9 @@
 
 
 def fused_kernel(
-    offs, acts, top, keys, vals, gain, acts_out, k_out, v_out,
+    offs, acts, top, keys, vals, gains, acts_out, k_out, v_out,
     q_in, up_s, k_in, v_in, g_in, grad, kk, vt, bias, sc, ex, dp, dkv, q2_s,
-    outgoing, from_core, part, from_chip, total, send, recv, ready,
+    outgoing, from_core, part, from_chip, total, gain, send, recv, ready,
 ):
     section, seq = lax.axis_index("section"), lax.axis_index("seq")
     core, chip = lax.rem(section, 2), lax.div(section, 2)
@@ -163,6 +167,7 @@
     partner = seq + 1 - 2 * lax.rem(seq, 2)
     x, y, z = lax.div(seq, 8), lax.rem(lax.div(seq, 4), 2), lax.rem(seq, 4)
     side = side_of(z)
+    turn = lax.rem(x + z, TILES)
     mine = rows_of(group * RB, RB)
 
     barrier = pltpu.get_barrier_semaphore()
@@ -174,6 +179,8 @@
     lax.fori_loop(1, SEQ, hello, 0)
     for j in range(1, SECT):
         pl.semaphore_signal(barrier, inc=1, device_id=(lax.rem(section + j, SECT), seq), device_id_type=MESH)
+    for up in range(2):
+        gain[up] = jnp.broadcast_to(gains[:, columns(head_at(2 * up, seq))], (8, DH))
     fill_bias(offs, group * RB, bias)
     dkv[...] = jnp.zeros_like(dkv)
     pl.semaphore_wait(barrier, SEQ + SECT - 2)
@@ -222,11 +229,11 @@
     keep(gain.at[chip], g_in.at[section], recv.at[7])
     pl.semaphore_wait(ready, SECT - 1)
 
+    lax.fori_loop(1, SEQ, send_cached, 0)
     @pl.when(section == SECT - 1)
     def _():
         send_queries()
 
-    lax.fori_loop(1, SEQ, send_cached, 0)
     for j in range(1, SECT):
         to_section = lax.rem(section + j, SECT)
         push(gain.at[lax.div(to_section, 2)], g_in.at[section], send.at[4], recv.at[7], (to_section, seq))
@@ -250,40 +257,48 @@
     vt[...] = v_in[...].T
     arrived(g_in, recv.at[7])
     arrived(q_in.at[pl.ds((SECT - 1) * SEQ, SEQ)], recv.at[3 + SECT - 1])
-    q2_s[...] = split_query(load_query(q_in, g_in, 0))
-    peak = jnp.max(scores(0, 0, kk, q2_s, bias, sc), axis=1, keepdims=True)
+    q2_s[...] = split_query(load_query(q_in, g_in, 0, turn))
+    peak = jnp.max(scores(turn, 0, kk, q2_s, bias, sc), axis=1, keepdims=True)
     arrived(up_s, recv.at[2])
 
+    def send_grads(step):
+        layer, t = at_step(step, turn)
+        first = layer * SEQ + t * GRP
+
+        def send_one(inside):
+            push(
+                grad.at[first + inside], acts_out.at[mine, columns(head)],
+                send.at[7], recv.at[10], (layer, t * GRP + inside),
+            )
+
+        for k in range(1, GRP):
+            send_one(lax.rem(seq + k, GRP))
+        inside = lax.rem(seq, GRP)
+        own = (layer == section) & (t == lax.div(seq, GRP))
+
+        @pl.when(own)
+        def _():
+            keep(grad.at[first + inside], acts_out.at[mine, columns(head)], recv.at[10])
+
+        @pl.when(jnp.logical_not(own))
+        def _():
+            send_one(inside)
+
     def attend(step, peak):
-        layer, t = SECT - 1 - lax.div(step, TILES), lax.rem(step, TILES)
-
-        @pl.when((t == TILES - 1) & (layer > 0))
+        layer = SECT - 1 - lax.div(step, TILES)
+
+        @pl.when((lax.rem(step, TILES) == TILES - 1) & (layer > 0))
         def _():
             arrived(q_in.at[pl.ds((layer - 1) * SEQ, SEQ)], recv.at[2 + layer])
 
-        peak = one_step(step, peak, q_in, g_in, k_in, grad, kk, vt, bias, sc, ex, dp, dkv, q2_s, up_s)
-
-        def send_grad(k, _):
-            block = t * GRP + k
-            own = (layer == section) & (block == seq)
-
-            @pl.when(own)
-            def _():
-                keep(grad.at[layer * SEQ + block], acts_out.at[mine, columns(head)], recv.at[10])
-
-            @pl.when(jnp.logical_not(own))
-            def _():
-                push(
-                    grad.at[layer * SEQ + block], acts_out.at[mine, columns(head)],
-                    send.at[7], recv.at[10], (layer, block),
-                )
-
-            return 0
-
-        lax.fori_loop(0, GRP, send_grad, 0)
+        return one_step(step, turn, peak, q_in, g_in, k_in, grad, kk, vt, bias, sc, ex, dp, dkv, q2_s, up_s)
+
+    def attend_send(step, peak):
+        peak = attend(step, peak)
+        send_grads(step)
         return peak
 
-    lax.fori_loop(0, STEPS, attend, peak)
+    lax.fori_loop(0, STEPS, attend_send, peak)
 
     near_half = pl.ds(pl.multiple_of(core * KHALF, DH), KHALF)
     far_half = pl.ds(pl.multiple_of((1 - core) * KHALF, DH), KHALF)
@@ -310,7 +325,7 @@
 
     def send_totals(kv, p, target):
         def some(i, _):
-            which = lax.rem(2 * x + i, PBLOCKS)
+            which = lax.rem(2 * (x + z) + section + i, PBLOCKS)
             block = block_at(lax.rem(y + p, 2), which, side)
             src = total.at[kv, rows_of(piece(p) + which * HALF, HALF)]
 
@@ -358,7 +373,7 @@
         arrived(out.at[core], send.at[13 + kv])
 
 
-def attention_grads(offs, acts, top, keys, vals, gain):
+def attention_grads(offs, acts, top, keys, vals, gains):
     bf = jnp.bfloat16
     any_space = pl.BlockSpec(memory_space=pl.ANY)
     return pl.pallas_call(
@@ -368,7 +383,7 @@
             jax.ShapeDtypeStruct((2, HALF, SEQ * DH), bf),
             jax.ShapeDtypeStruct((2, HALF, SEQ * DH), bf),
         ),
-        in_specs=[pl.BlockSpec(memory_space=pltpu.SMEM)] + [any_space] * 5,
+        in_specs=[pl.BlockSpec(memory_space=pltpu.SMEM)] + [any_space] * 4 + [pl.BlockSpec(memory_space=pltpu.VMEM)],
         out_specs=(any_space, any_space, any_space),
         scratch_shapes=[
             pltpu.VMEM((ALL, RB, DH), bf),
@@ -390,6 +405,7 @@
             pltpu.VMEM((2, KHALF, DH), bf),
             pltpu.VMEM((2, SIDE, DH), bf),
             pltpu.VMEM((2, SIDE, DH), bf),
+            pltpu.VMEM((2, 8, DH), jnp.float32),
             pltpu.SemaphoreType.DMA((15,)),
             pltpu.SemaphoreType.DMA((21,)),
             pltpu.SemaphoreType.REGULAR,
@@ -397,16 +413,36 @@
         compiler_params=pltpu.CompilerParams(
             collective_id=0, has_side_effects=True, vmem_limit_bytes=60 * 2**20
         ),
-    )(offs, acts, top, keys, vals, gain)
+    )(offs, acts, top, keys, vals, gains)
+
+
+def store_kernel(a, b, c, a_out, b_out, c_out, sems):
+    copies = [
+        pltpu.make_async_copy(src, dst, sems.at[i])
+        for i, (src, dst) in enumerate(((a, a_out), (b, b_out), (c, c_out)))
+    ]
+    for copy in copies:
+        copy.start()
+    for copy in copies:
+        copy.wait()
+
+
+def store(*arrays):
+    any_space = pl.BlockSpec(memory_space=pl.ANY)
+    return pl.pallas_call(
+        store_kernel,
+        out_shape=tuple(jax.ShapeDtypeStruct(a.shape, a.dtype) for a in arrays),
+        in_specs=[pl.BlockSpec(memory_space=pltpu.VMEM)] * 3,
+        out_specs=(any_space,) * 3,
+        scratch_shapes=[pltpu.SemaphoreType.DMA((3,))],
+    )(*arrays)
 
 
 def local(acts, gains, grad_top, keys, values, offsets):
-    low_head = head_at(0, lax.axis_index("seq"))
-    slices = [lax.dynamic_slice(gains, (0, (low_head + step) * DH), (1, DH)) for step in (0, 2)]
-    gain = jnp.broadcast_to(jnp.stack(slices), (2, 8, DH))
     out_acts, out_keys, out_values = attention_grads(
-        offsets, acts[0], grad_top, keys.reshape(2, HALF, -1), values.reshape(2, HALF, -1), gain
+        offsets, acts[0], grad_top, keys.reshape(2, HALF, -1), values.reshape(2, HALF, -1), gains
     )
+    out_acts, out_keys, out_values = store(out_acts, out_keys, out_values)
     return (out_acts[None], out_keys.reshape(2 * HALF, -1), out_values.reshape(2 * HALF, -1))
 
 

time: 106 us -> 100 us (0.943)
  local copies, waits for them, and re-layouts: 5.94 us -> 0 us
    unnamed x7 -> x0, local copies, waits for them, and re-layouts: 4.66 us -> none
    pallas_call x0 -> x1, Pallas kernels: none -> 3.2 us  [store(): pl.pallas_call(store_kernel, out_shape=tuple((jax.ShapeDtypeStruct(a.shap...]
    pallas_call x1, Pallas kernels: 98.7 us -> 96.3 us  [attention_grads(): pl.pallas_call(fused_kernel, out_shape=(jax.ShapeDtypeStruct((SECT * RB,...]
where the time goes in v4:
time: 100 us
  Pallas kernels  99.5 us (100%)
    pallas_call x1, Pallas kernels, attention_grads(): pl.pallas_call(fused_kernel, out_shape=(jax.ShapeDtypeStruct((SECT * RB,...  96.3 us
    pallas_call x1, Pallas kernels, store(): pl.pallas_call(store_kernel, out_shape=tuple((jax.ShapeDtypeStruct(a.shap...  3.2 us

profile of v4, /device:TPU:1, one launch (start us, length us, event | category | flops | bytes accessed | tf_op | source)
XLA Modules:
  0.0 100.1 jit_solution(16920404814476552)
XLA Ops:
  0.6 96.3 %shard_map.85 = (bf16[128,4096]{1,0:T(8,128)(2,1)}, bf16[2,48,4096]{2,1,0:T(8,128)(2,1)}, bf16[2,48,4096]{2,1,0:T(8,128)(2,1)}) custom-call(s32[32]{0:T(128)} %offs.1, bf16[128,4096]{1,0:T(8,128)(2,1)} %bitcast.6, bf16[128,4096]{1,0:T(8,128)(2,1)} %top.1, bf16[2,48,4096]{2,1,0:T(8,128)(2,1)} %bitcast.7, bf16[2,48,4096]{2,1,0:T(8,128)(2,1)} %bitcast.8, ...), custom_call_target="tpu_custom_call" | custom-call | tf_op jit(solution)/shard_map/pallas_call | solution.py:379
  96.9 3.2 %shard_map.86 = (bf16[128,4096]{1,0:T(8,128)(2,1)}, bf16[2,48,4096]{2,1,0:T(8,128)(2,1)}, bf16[2,48,4096]{2,1,0:T(8,128)(2,1)}) custom-call(bf16[128,4096]{1,0:T(8,128)(2,1)} %get-tuple-element.9.a, bf16[2,48,4096]{2,1,0:T(8,128)(2,1)} %get-tuple-element.10.b, bf16[2,48,4096]{2,1,0:T(8,128)(2,1)} %get-tuple-element.11.c), custom_call_target="tpu_custom_call" | custom-call | tf_op jit(solution)/shard_map/pallas_call | solution.py:432

commit v5 on v4

--- a/solution.py
+++ b/solution.py
@@ -227,9 +227,9 @@
     keep(top_rows(seq), up_s.at[seq], recv.at[2])
     keep(query_rows(section, seq), q_in.at[me], recv.at[3 + section])
     keep(gain.at[chip], g_in.at[section], recv.at[7])
+
+    lax.fori_loop(1, SEQ, send_cached, 0)
     pl.semaphore_wait(ready, SECT - 1)
-
-    lax.fori_loop(1, SEQ, send_cached, 0)
     @pl.when(section == SECT - 1)
     def _():
         send_queries()
@@ -242,19 +242,19 @@
     k_other, v_other = k_in.at[rows_of((1 - core) * KHALF, KHALF)], v_in.at[rows_of((1 - core) * KHALF, KHALF)]
     arrived(k_half, recv.at[0])
     push(k_half, k_half, send.at[5], recv.at[8], (sibling, seq))
-    arrived(v_half, recv.at[1])
-    push(v_half, v_half, send.at[6], recv.at[9], (sibling, seq))
-
-    @pl.when(section != SECT - 1)
-    def _():
-        send_queries()
 
     arrived(k_other, recv.at[8])
     kt = k_in[...].T
     kk[:DH, :] = kt
     kk[DH:, :] = kt
+    arrived(v_half, recv.at[1])
+    push(v_half, v_half, send.at[6], recv.at[9], (sibling, seq))
     arrived(v_other, recv.at[9])
     vt[...] = v_in[...].T
+    @pl.when(section != SECT - 1)
+    def _():
+        send_queries()
+
     arrived(g_in, recv.at[7])
     arrived(q_in.at[pl.ds((SECT - 1) * SEQ, SEQ)], recv.at[3 + SECT - 1])
     q2_s[...] = split_query(load_query(q_in, g_in, 0, turn))

time: 100 us -> 96.3 us (0.963)
  Pallas kernels: 99.5 us -> 95.4 us
    pallas_call x1, Pallas kernels: 96.3 us -> 92.2 us  [attention_grads(): pl.pallas_call(fused_kernel, out_shape=(jax.ShapeDtypeStruct((SECT * RB,...]
where the time goes in v5:
time: 96.3 us; the launch traced here: 96.1 us
  Pallas kernels  95.4 us (99%)
    pallas_call x1, Pallas kernels, attention_grads(): pl.pallas_call(fused_kernel, out_shape=(jax.ShapeDtypeStruct((SECT * RB,...  92.2 us
    pallas_call x1, Pallas kernels, store(): pl.pallas_call(store_kernel, out_shape=tuple((jax.ShapeDtypeStruct(a.shap...  3.2 us

profile of v5, /device:TPU:1, one launch (start us, length us, event | category | flops | bytes accessed | tf_op | source)
XLA Modules:
  0.0 96.1 jit_solution(17731818210022651498)
XLA Ops:
  0.6 92.2 %shard_map.85 = (bf16[128,4096]{1,0:T(8,128)(2,1)}, bf16[2,48,4096]{2,1,0:T(8,128)(2,1)}, bf16[2,48,4096]{2,1,0:T(8,128)(2,1)}) custom-call(s32[32]{0:T(128)} %offs.1, bf16[128,4096]{1,0:T(8,128)(2,1)} %bitcast.6, bf16[128,4096]{1,0:T(8,128)(2,1)} %top.1, bf16[2,48,4096]{2,1,0:T(8,128)(2,1)} %bitcast.7, bf16[2,48,4096]{2,1,0:T(8,128)(2,1)} %bitcast.8, ...), custom_call_target="tpu_custom_call" | custom-call | tf_op jit(solution)/shard_map/pallas_call | solution.py:379
  92.9 3.2 %shard_map.86 = (bf16[128,4096]{1,0:T(8,128)(2,1)}, bf16[2,48,4096]{2,1,0:T(8,128)(2,1)}, bf16[2,48,4096]{2,1,0:T(8,128)(2,1)}) custom-call(bf16[128,4096]{1,0:T(8,128)(2,1)} %get-tuple-element.9.a, bf16[2,48,4096]{2,1,0:T(8,128)(2,1)} %get-tuple-element.10.b, bf16[2,48,4096]{2,1,0:T(8,128)(2,1)} %get-tuple-element.11.c), custom_call_target="tpu_custom_call" | custom-call | tf_op jit(solution)/shard_map/pallas_call | solution.py:432

commit v6 on v5

--- a/solution.py
+++ b/solution.py
@@ -416,15 +416,23 @@
     )(offs, acts, top, keys, vals, gains)
 
 
-def store_kernel(a, b, c, a_out, b_out, c_out, sems):
-    copies = [
-        pltpu.make_async_copy(src, dst, sems.at[i])
-        for i, (src, dst) in enumerate(((a, a_out), (b, b_out), (c, c_out)))
-    ]
-    for copy in copies:
-        copy.start()
-    for copy in copies:
-        copy.wait()
+def store_kernel(a, b, c, a_out, b_out, c_out, a_tmp, b_tmp, c_tmp, sems):
+    parts = []
+    for src, tmp, dst in ((a, a_tmp, a_out), (b, b_tmp, b_out), (c, c_tmp, c_out)):
+        half = src.shape[1] // 2
+        for cols in (slice(0, half), slice(half, 2 * half)):
+            n = len(parts)
+            parts.append((
+                pltpu.make_async_copy(src.at[:, cols], tmp.at[:, cols], sems.at[0, n]),
+                pltpu.make_async_copy(tmp.at[:, cols], dst.at[:, cols], sems.at[1, n]),
+            ))
+    for load, _ in parts:
+        load.start()
+    for load, save in parts:
+        load.wait()
+        save.start()
+    for _, save in parts:
+        save.wait()
 
 
 def store(*arrays):
@@ -432,9 +440,9 @@
     return pl.pallas_call(
         store_kernel,
         out_shape=tuple(jax.ShapeDtypeStruct(a.shape, a.dtype) for a in arrays),
-        in_specs=[pl.BlockSpec(memory_space=pltpu.VMEM)] * 3,
+        in_specs=[any_space] * 3,
         out_specs=(any_space,) * 3,
-        scratch_shapes=[pltpu.SemaphoreType.DMA((3,))],
+        scratch_shapes=[pltpu.VMEM(a.shape, a.dtype) for a in arrays] + [pltpu.SemaphoreType.DMA((2, 6))],
     )(*arrays)
 
 
@@ -442,8 +450,10 @@
     out_acts, out_keys, out_values = attention_grads(
         offsets, acts[0], grad_top, keys.reshape(2, HALF, -1), values.reshape(2, HALF, -1), gains
     )
-    out_acts, out_keys, out_values = store(out_acts, out_keys, out_values)
-    return (out_acts[None], out_keys.reshape(2 * HALF, -1), out_values.reshape(2 * HALF, -1))
+    out_acts, out_keys, out_values = store(
+        out_acts, out_keys.reshape(2 * HALF, -1), out_values.reshape(2 * HALF, -1)
+    )
+    return (out_acts[None], out_keys, out_values)
 
 
 def solution(mesh):

time: 96.3 us -> 95.7 us (level)
  no operation moved by 1% of the time
where the time goes in v6:
time: 95.7 us; the launch traced here: 95.5 us
  Pallas kernels  94.8 us (99%)
    pallas_call x1, Pallas kernels, attention_grads(): pl.pallas_call(fused_kernel, out_shape=(jax.ShapeDtypeStruct((SECT * RB,...  92.2 us
    pallas_call x1, Pallas kernels, store(): pl.pallas_call(store_kernel, out_shape=tuple((jax.ShapeDtypeStruct(a.shap...  2.63 us

profile of v6, /device:TPU:1, one launch (start us, length us, event | category | flops | bytes accessed | tf_op | source)
XLA Modules:
  0.0 95.5 jit_solution(9854497457551691073)
XLA Ops:
  0.6 92.2 %shard_map.85 = (bf16[128,4096]{1,0:T(8,128)(2,1)}, bf16[2,48,4096]{2,1,0:T(8,128)(2,1)}, bf16[2,48,4096]{2,1,0:T(8,128)(2,1)}) custom-call(s32[32]{0:T(128)} %offs.1, bf16[128,4096]{1,0:T(8,128)(2,1)} %bitcast.6, bf16[128,4096]{1,0:T(8,128)(2,1)} %top.1, bf16[2,48,4096]{2,1,0:T(8,128)(2,1)} %bitcast.9, bf16[2,48,4096]{2,1,0:T(8,128)(2,1)} %bitcast.10, ...), custom_call_target="tpu_custom_call" | custom-call | tf_op jit(solution)/shard_map/pallas_call | solution.py:379
  92.9 2.6 %shard_map.86 = (bf16[128,4096]{1,0:T(8,128)(2,1)}, bf16[96,4096]{1,0:T(8,128)(2,1)}, bf16[96,4096]{1,0:T(8,128)(2,1)}) custom-call(bf16[128,4096]{1,0:T(8,128)(2,1)} %get-tuple-element.9.a, bf16[96,4096]{1,0:T(8,128)(2,1)} %bitcast.7, bf16[96,4096]{1,0:T(8,128)(2,1)} %bitcast.8), custom_call_target="tpu_custom_call" | custom-call | tf_op jit(solution)/shard_map/pallas_call | solution.py:440

commit v7 on v6

--- a/solution.py
+++ b/solution.py
@@ -304,7 +304,9 @@
     far_half = pl.ds(pl.multiple_of((1 - core) * KHALF, DH), KHALF)
     for kv in range(2):
         outgoing[kv] = dkv[kv, :, far_half].astype(jnp.bfloat16).T
-        push(outgoing.at[kv], from_core.at[kv], send.at[8 + kv], recv.at[11 + kv], (sibling, seq))
+        for far, sem in ((1 - side, 11 + kv), (side, 21 + kv)):
+            rows = rows_of(far * SIDE, SIDE)
+            push(outgoing.at[kv, rows], from_core.at[kv, rows], send.at[8 + kv], recv.at[sem], (sibling, seq))
 
     def add_core(kv, rows):
         return part[kv, rows].astype(jnp.float32) + from_core[kv, rows].astype(jnp.float32)
@@ -314,7 +316,7 @@
 
     for kv in range(2):
         part[kv] = dkv[kv, :, near_half].astype(jnp.bfloat16).T
-        arrived(from_core.at[kv], recv.at[11 + kv])
+        arrived(from_core.at[kv, rows_of((1 - side) * SIDE, SIDE)], recv.at[11 + kv])
         for p in range(2):
             rows = rows_of((1 - side) * SIDE + piece(p), PROWS)
             part[kv, rows] = add_core(kv, rows).astype(jnp.bfloat16)
@@ -345,6 +347,8 @@
     for kv, out in ((0, k_out), (1, v_out)):
         for p in range(2):
             done = rows_of(piece(p), PROWS)
+            if p == 0:
+                arrived(from_core.at[kv, rows_of(side * SIDE, SIDE)], recv.at[21 + kv])
             arrived(from_chip.at[kv, done], recv.at[13 + 2 * kv + p])
             total[kv, done] = (
                 add_core(kv, rows_of(side * SIDE + piece(p), PROWS)) + from_chip[kv, done].astype(jnp.float32)
@@ -407,7 +411,7 @@
             pltpu.VMEM((2, SIDE, DH), bf),
             pltpu.VMEM((2, 8, DH), jnp.float32),
             pltpu.SemaphoreType.DMA((15,)),
-            pltpu.SemaphoreType.DMA((21,)),
+            pltpu.SemaphoreType.DMA((23,)),
             pltpu.SemaphoreType.REGULAR,
         ],
         compiler_params=pltpu.CompilerParams(

time: 95.7 us -> 95.5 us (level)
  no operation moved by 1% of the time
where the time goes in v7:
time: 95.5 us; the launch traced here: 95.3 us
  Pallas kernels  94.7 us (99%)
    pallas_call x1, Pallas kernels, attention_grads(): pl.pallas_call(fused_kernel, out_shape=(jax.ShapeDtypeStruct((SECT * RB,...  92 us
    pallas_call x1, Pallas kernels, store(): pl.pallas_call(store_kernel, out_shape=tuple((jax.ShapeDtypeStruct(a.shap...  2.63 us

profile of v7, /device:TPU:1, one launch (start us, length us, event | category | flops | bytes accessed | tf_op | source)
XLA Modules:
  0.0 95.3 jit_solution(5071425559321455865)
XLA Ops:
  0.6 92.0 %shard_map.85 = (bf16[128,4096]{1,0:T(8,128)(2,1)}, bf16[2,48,4096]{2,1,0:T(8,128)(2,1)}, bf16[2,48,4096]{2,1,0:T(8,128)(2,1)}) custom-call(s32[32]{0:T(128)} %offs.1, bf16[128,4096]{1,0:T(8,128)(2,1)} %bitcast.6, bf16[128,4096]{1,0:T(8,128)(2,1)} %top.1, bf16[2,48,4096]{2,1,0:T(8,128)(2,1)} %bitcast.9, bf16[2,48,4096]{2,1,0:T(8,128)(2,1)} %bitcast.10, ...), custom_call_target="tpu_custom_call" | custom-call | tf_op jit(solution)/shard_map/pallas_call | solution.py:383
  92.7 2.6 %shard_map.86 = (bf16[128,4096]{1,0:T(8,128)(2,1)}, bf16[96,4096]{1,0:T(8,128)(2,1)}, bf16[96,4096]{1,0:T(8,128)(2,1)}) custom-call(bf16[128,4096]{1,0:T(8,128)(2,1)} %get-tuple-element.9.a, bf16[96,4096]{1,0:T(8,128)(2,1)} %bitcast.7, bf16[96,4096]{1,0:T(8,128)(2,1)} %bitcast.8), custom_call_target="tpu_custom_call" | custom-call | tf_op jit(solution)/shard_map/pallas_call | solution.py:444
